TPU v7x, 32 devices: a whole 2x2x4 slice. The times are simulated.
32 devices in a mesh: frame: 16 (over z, y, core), rep: 2 (over x).
Axes of the slice: x: 2, y: 2, z: 4, core: 2. Of those that a mesh axis runs over, the one named last changes fastest.
Arguments:
- clean: float32 [2, 16, 16, 256], P('rep', 'frame'), may hold values from -6 to 6
- noise: float32 [2, 16, 16, 256], P('rep', 'frame'), may hold values from -6 to 6
- levels: int32 [2, 16], P('rep', 'frame'), may hold values from 1 to 31
- flags: int32 [2, 16], P('rep', 'frame'), may hold values 0 or 1
- frame_map: int32 [2, 16], replicated, may hold values from 0 to 15, each once within a row
- block_slot: int32 [768], replicated, may hold values from 0 to 767, each once
- step_count: int32 [1], replicated, may hold values from 2 to 20
- mat_weight: float32 [768, 128, 128], P(('frame', 'rep')), may hold values from -0.1875 to 0.1875
- mat_ema: float32 [768, 128, 128], P(('frame', 'rep')), may hold values from -0.1875 to 0.1875
- stat_left: float32 [768, 128, 128], P(('frame', 'rep')), as said below
- stat_right: float32 [768, 128, 128], P(('frame', 'rep')), as said below
- root_left: float32 [768, 128, 128], P(('frame', 'rep')), as said below
- root_right: float32 [768, 128, 128], P(('frame', 'rep')), as said below
- mod_table: float32 [32, 8192], replicated, may hold values from -3 to 3
- mod_mom: float32 [32, 8192], replicated, may hold values from -2.670288e-05 to 2.670288e-05
- mod_var: float32 [32, 8192], replicated, may hold values from 1.6895545e-13 to 1.3516436e-12
- mod_ema: float32 [32, 8192], replicated, may hold values from -3 to 3
- io_weight: float32 [33, 1024], replicated, may hold values from -0.75 to 0.75
- io_mom: float32 [33, 1024], replicated, may hold values from -0.00030517578 to 0.00030517578
- io_var: float32 [33, 1024], replicated, may hold values from 1.6895546e-11 to 2.7032873e-10
- io_ema: float32 [33, 1024], replicated, may hold values from -0.75 to 0.75
Outputs:
- loss_sum: float32 [], replicated
- noised_count: float32 [], replicated
- grad_norm: float32 [], replicated
- mat_grad: float32 [768, 128, 128], P(('frame', 'rep'))
- new_mat_weight: float32 [768, 128, 128], P(('frame', 'rep'))
- new_stat_left: float32 [768, 128, 128], P(('frame', 'rep'))
- new_stat_right: float32 [768, 128, 128], P(('frame', 'rep'))
- new_mat_ema: float32 [768, 128, 128], P(('frame', 'rep'))
- new_mod_table: float32 [32, 8192], replicated
- new_mod_mom: float32 [32, 8192], replicated
- new_mod_var: float32 [32, 8192], replicated
- new_mod_ema: float32 [32, 8192], replicated
- new_io_weight: float32 [33, 1024], replicated
- new_io_mom: float32 [33, 1024], replicated
- new_io_var: float32 [33, 1024], replicated
- new_io_ema: float32 [33, 1024], replicated
Inputs may be any that keep to these rules, and one draw needn't show every extreme that they name: `stat_left`: symmetric blocks with positive diagonal, each strictly diagonally dominant. `stat_right`: symmetric blocks with positive diagonal, each strictly diagonally dominant. `root_left`: symmetric blocks with positive diagonal, each strictly diagonally dominant. `root_right`: symmetric blocks with positive diagonal, each strictly diagonally dominant.
All inputs are finite; a program needn't handle non-finite values. No bound on the sum of `flags` on one device may be relied on, other than what follows from the above.
Results may differ from a plain program's by a relative error of at most 0.01.
Values may be sent and summed in bfloat16 or wider, within the bound.
A program may use at most 640 MiB of HBM per device.

v0:
```python
from functools import partial
import math

import jax
import jax.numpy as jnp
from jax import lax
from jax.sharding import PartitionSpec as P

D = 1024
HEADS = 16
HEAD_DIM = 64
FFN = 4096
PIN = 16
GRID = 16
BLOCK = 128
LEVELS = 32
FR_DEV = 1
NPARAMS = 12878848


LN_EPS = 1e-06
ROPE_BASE = 10000.0
CLIP_NORM = 0.01
BETA_ONE = 0.9
BETA_TWO = 0.999
ADAM_EPS = 1e-08
ADAM_RATE = 0.1
DECAY_RATE = 0.1
STAT_BETA = 0.95
SHAMPOO_RATE = 0.01
EMA_DECAY = 0.9
TOP_PRECISION = lax.Precision.HIGHEST


def matmul(left, right):
    return jnp.dot(left, right, preferred_element_type=jnp.float32)


def layer_norm(hidden):
    centered = hidden - jnp.mean(hidden, axis=-1, keepdims=True)
    inverse = lax.rsqrt(jnp.mean(centered * centered, axis=-1, keepdims=True) + LN_EPS)
    return (centered * inverse, inverse)


def norm_back(grad_hat, normed, inverse):
    return inverse * (
        grad_hat
        - jnp.mean(grad_hat, axis=-1, keepdims=True)
        - normed * jnp.mean(grad_hat * normed, axis=-1, keepdims=True)
    )


def gelu_back(upper, grad_act):
    return jax.vjp(partial(jax.nn.gelu, approximate=True), upper)[1](grad_act)[0]


def frequencies(width):
    return ROPE_BASE ** (-jnp.arange(width, dtype=jnp.float32) / width)


def rope_tables(frame_ids):
    pairs = HEAD_DIM // 2
    time_pairs = pairs // 4
    row_pairs = (pairs - time_pairs) // 2
    column_pairs = pairs - time_pairs - row_pairs
    frames = frame_ids.shape[0]
    tok_frame = GRID * GRID
    token_pos = jnp.arange(tok_frame, dtype=jnp.int32)
    row_pos = (token_pos // GRID).astype(jnp.float32)
    column_pos = (token_pos % GRID).astype(jnp.float32)
    time_angle = (
        frame_ids.astype(jnp.float32)[:, None, None] * frequencies(time_pairs)[None, None, :]
    )
    row_angle = row_pos[None, :, None] * frequencies(row_pairs)[None, None, :]
    column_angle = column_pos[None, :, None] * frequencies(column_pairs)[None, None, :]
    angles = jnp.concatenate(
        [jnp.broadcast_to(time_angle, (frames, tok_frame, time_pairs)), row_angle, column_angle],
        axis=-1,
    )
    angles = angles.reshape(frames * tok_frame, pairs)
    return (jnp.cos(angles), jnp.sin(angles))


def rotate(values, cosine, sine):
    pairs = HEAD_DIM // 2
    first, second = (values[..., :pairs], values[..., pairs:])
    cosine = cosine[:, None, :]
    sine = sine[:, None, :]
    return jnp.concatenate(
        [first * cosine - second * sine, first * sine + second * cosine], axis=-1
    )


def split_heads(flat):
    return flat.reshape(flat.shape[0], HEADS, HEAD_DIM)


def matrix_shapes():
    return ((D, 3 * D), (D, D), (D, FFN), (FFN, D))


def from_blocks(natural):
    matrices = []
    offset = 0
    for rows_in, cols_in in matrix_shapes():
        count_in = rows_in // BLOCK * (cols_in // BLOCK)
        part_blocks = natural[offset : offset + count_in]
        matrices.append(
            part_blocks.reshape(rows_in // BLOCK, cols_in // BLOCK, BLOCK, BLOCK)
            .transpose(0, 2, 1, 3)
            .reshape(rows_in, cols_in)
        )
        offset = offset + count_in
    return matrices


def to_blocks(matrix):
    rows_in, cols_in = matrix.shape
    return (
        matrix.reshape(rows_in // BLOCK, BLOCK, cols_in // BLOCK, BLOCK)
        .transpose(0, 2, 1, 3)
        .reshape(-1, BLOCK, BLOCK)
    )


def score_block(queries, key_block, query_frames, key_frames):
    scores = jnp.einsum(
        "qhd,khd->hqk", queries, key_block, preferred_element_type=jnp.float32
    ) * HEAD_DIM ** (-0.5)
    visible = key_frames[None, None, :] <= query_frames[None, :, None]
    return jnp.where(visible, scores, -jnp.inf)


def stack_keys(key_rows, value_rows, frame_rows):
    total_rows = key_rows.shape[0]
    block_rows = math.gcd(total_rows, 512)
    blocks = total_rows // block_rows
    return (
        (
            key_rows.reshape(blocks, block_rows, HEADS, HEAD_DIM),
            value_rows.reshape(blocks, block_rows, HEADS, HEAD_DIM),
            frame_rows.reshape(blocks, block_rows),
        ),
        block_rows,
    )


def keep_state(previous):
    return previous


def fold_keys(state, shard_rows, queries, query_frames, key_frames_all):
    key_rows, value_rows = shard_rows
    stacks, block_rows = stack_keys(key_rows, value_rows, key_frames_all)
    top_query = jnp.max(query_frames)

    def fold_step_block(carried, block_in):
        key_block, value_block, key_frames = block_in

        def fold_compute(previous):
            running, denominator, accumulated = previous
            scores = score_block(queries, key_block, query_frames, key_frames)
            new_max = jnp.maximum(running, jnp.max(scores, axis=-1))
            weights = jnp.exp(scores - new_max[..., None])
            rescale = jnp.exp(running - new_max)
            contrib = jnp.einsum(
                "hqk,khd->hqd",
                weights.astype(jnp.bfloat16),
                value_block,
                preferred_element_type=jnp.float32,
            )
            return (
                new_max,
                denominator * rescale + jnp.sum(weights, axis=-1),
                accumulated * rescale[..., None] + contrib,
            )

        return (lax.cond(jnp.min(key_frames) <= top_query, fold_compute, keep_state, carried), None)

    state, unused = lax.scan(fold_step_block, state, stacks)
    return state


def grad_parts(
    queries, grad_heads, delta, log_total, query_frames, key_block, value_block, key_frames
):
    probs = jnp.exp(
        score_block(queries, key_block, query_frames, key_frames) - log_total[..., None]
    )
    grad_probs = jnp.einsum(
        "qhd,khd->hqk", grad_heads, value_block, preferred_element_type=jnp.float32
    )
    grad_scores = (probs * (grad_probs - delta[..., None])).astype(jnp.bfloat16)
    return (probs, grad_scores)


def key_value_block(
    queries, grad_heads, delta, log_total, query_frames, key_block, value_block, key_frames
):
    block_rows = key_block.shape[0]
    probs, grad_scores = grad_parts(
        queries, grad_heads, delta, log_total, query_frames, key_block, value_block, key_frames
    )
    key_grad = jnp.einsum(
        "hqk,qhd->khd", grad_scores, queries, preferred_element_type=jnp.float32
    ) * HEAD_DIM ** (-0.5)
    value_grad = jnp.einsum(
        "hqk,qhd->khd", probs.astype(jnp.bfloat16), grad_heads, preferred_element_type=jnp.float32
    )
    return jnp.concatenate(
        [key_grad.reshape(block_rows, D), value_grad.reshape(block_rows, D)], axis=1
    )


def query_grads(
    queries, grad_heads, delta, log_total, query_frames, key_all, value_all, key_frames_all
):
    stacks, block_rows = stack_keys(key_all, value_all, key_frames_all)
    top_query = jnp.max(query_frames)

    def query_step_block(carried, block_in):
        key_block, value_block, key_frames = block_in

        def query_compute(previous):
            probs, grad_scores = grad_parts(
                queries,
                grad_heads,
                delta,
                log_total,
                query_frames,
                key_block,
                value_block,
                key_frames,
            )
            return previous + jnp.einsum(
                "hqk,khd->qhd", grad_scores, key_block, preferred_element_type=jnp.float32
            )

        return (
            lax.cond(jnp.min(key_frames) <= top_query, query_compute, keep_state, carried),
            None,
        )

    initial = jnp.zeros(queries.shape, jnp.float32)
    result, unused = lax.scan(query_step_block, initial, stacks)
    return result * HEAD_DIM ** (-0.5)


def key_terms(
    row_count,
    queries,
    grad_heads,
    delta,
    log_total,
    query_frames,
    key_all,
    value_all,
    key_frames_all,
):
    stacks, block_rows = stack_keys(key_all, value_all, key_frames_all)
    top_query = jnp.max(query_frames)

    def one_block(block_in):
        key_block, value_block, key_frames = block_in

        def one_compute(unused):
            return key_value_block(
                queries,
                grad_heads,
                delta,
                log_total,
                query_frames,
                key_block,
                value_block,
                key_frames,
            )

        def nothing(unused):
            return jnp.zeros((block_rows, 2 * D), jnp.float32)

        return lax.cond(jnp.min(key_frames) <= top_query, one_compute, nothing, 0)

    return lax.map(one_block, stacks).reshape(row_count, 2 * D)


def shampoo(grads, weights, average, left, right, left_root, right_root):
    new_left = STAT_BETA * left + (1 - STAT_BETA) * jnp.einsum(
        "bij,bkj->bik", grads, grads, precision=TOP_PRECISION
    )
    new_right = STAT_BETA * right + (1 - STAT_BETA) * jnp.einsum(
        "bji,bjk->bik", grads, grads, precision=TOP_PRECISION
    )
    direction = jnp.einsum("bij,bjk->bik", left_root, grads, precision=TOP_PRECISION)
    direction = jnp.einsum("bij,bjk->bik", direction, right_root, precision=TOP_PRECISION)
    direction = direction * lax.rsqrt(
        jnp.mean(direction * direction, axis=(1, 2), keepdims=True) + 1e-06
    )
    new_weights = weights - SHAMPOO_RATE * (direction + DECAY_RATE * weights)
    new_average = EMA_DECAY * average + (1 - EMA_DECAY) * new_weights
    return (new_weights, new_left, new_right, new_average)


def adamw(grads, weights, first, second, average, step):
    new_first = BETA_ONE * first + (1 - BETA_ONE) * grads
    new_second = BETA_TWO * second + (1 - BETA_TWO) * grads * grads
    first_hat = new_first / (1 - BETA_ONE**step)
    second_hat = new_second / (1 - BETA_TWO**step)
    new_weights = weights - ADAM_RATE * (
        first_hat / (jnp.sqrt(second_hat) + ADAM_EPS) + DECAY_RATE * weights
    )
    new_average = EMA_DECAY * average + (1 - EMA_DECAY) * new_weights
    return (new_weights, new_first, new_second, new_average)


def on_device(
    clean,
    noise,
    levels,
    flags,
    frame_map,
    block_slot,
    step_count,
    mat_weight,
    mat_ema,
    stat_left,
    stat_right,
    root_left,
    root_right,
    mod_table,
    mod_mom,
    mod_var,
    mod_ema,
    io_weight,
    io_mom,
    io_var,
    io_ema,
):
    tok_frame = GRID * GRID
    local_rows = FR_DEV * tok_frame
    noised = (1 - flags[0]).astype(jnp.float32)
    noised_total = jnp.maximum(lax.psum(jnp.sum(noised), ("frame", "rep")), 1.0)
    gathered = lax.all_gather(mat_weight.astype(jnp.bfloat16), ("frame", "rep"), axis=0, tiled=True)
    natural = jnp.zeros_like(gathered).at[block_slot].set(gathered)
    attn_w, out_w, up_w, down_w = from_blocks(natural)
    clip_map = lax.dynamic_index_in_dim(frame_map, lax.axis_index("rep"), 0, keepdims=False)
    my_frames = lax.dynamic_slice_in_dim(clip_map, lax.axis_index("frame") * FR_DEV, FR_DEV)
    key_frames_all = jnp.repeat(clip_map, tok_frame)
    query_frames = jnp.repeat(my_frames, tok_frame)
    level_now = levels[0] * (1 - flags[0])
    fraction = level_now.astype(jnp.float32) / LEVELS
    keep_coef = jnp.cos(0.5 * jnp.pi * fraction)
    noise_coef = jnp.sin(0.5 * jnp.pi * fraction)
    frames_in = keep_coef[:, None, None] * clean[0] + noise_coef[:, None, None] * noise[0]
    inputs = jnp.swapaxes(frames_in, 1, 2).reshape(local_rows, PIN).astype(jnp.bfloat16)
    targets = jnp.swapaxes(noise[0], 1, 2).reshape(local_rows, PIN)
    selector = (level_now[:, None] == jnp.arange(LEVELS, dtype=jnp.int32)[None, :]).astype(
        jnp.float32
    )
    modulation = jnp.dot(selector, mod_table, precision=TOP_PRECISION).reshape(FR_DEV, 8, 1, D)
    io_low = io_weight.astype(jnp.bfloat16)
    embed = io_low[:PIN]
    head = io_low[PIN : 2 * PIN]
    start = (matmul(inputs, embed) + io_weight[2 * PIN]).reshape(FR_DEV, tok_frame, D)
    hat_one, inv_one = layer_norm(start)
    normed = (
        (hat_one * (1 + modulation[:, 1]) + modulation[:, 0])
        .reshape(local_rows, D)
        .astype(jnp.bfloat16)
    )
    projected = matmul(normed, attn_w)
    cosine, sine = rope_tables(my_frames)
    queries = rotate(split_heads(projected[:, :D]), cosine, sine).astype(jnp.bfloat16)
    key_flat = (
        rotate(split_heads(projected[:, D : 2 * D]), cosine, sine)
        .astype(jnp.bfloat16)
        .reshape(local_rows, D)
    )
    value_flat = projected[:, 2 * D :].astype(jnp.bfloat16)
    initial = (
        jnp.full((HEADS, local_rows), -1e30, jnp.float32),
        jnp.zeros((HEADS, local_rows), jnp.float32),
        jnp.zeros((HEADS, local_rows, HEAD_DIM), jnp.float32),
    )
    running, denominator, accumulated = fold_keys(
        initial,
        (
            lax.all_gather(key_flat, "frame", axis=0, tiled=True),
            lax.all_gather(value_flat, "frame", axis=0, tiled=True),
        ),
        queries,
        query_frames,
        key_frames_all,
    )
    attended = jnp.transpose(accumulated / denominator[..., None], (1, 0, 2)).reshape(local_rows, D)
    log_total = running + jnp.log(denominator)
    attended_low = attended.astype(jnp.bfloat16)
    branch = matmul(attended_low, out_w).reshape(FR_DEV, tok_frame, D)
    middle = start + modulation[:, 2] * branch
    hat_two, inv_two = layer_norm(middle)
    normed_two = (
        (hat_two * (1 + modulation[:, 4]) + modulation[:, 3])
        .reshape(local_rows, D)
        .astype(jnp.bfloat16)
    )
    upper = matmul(normed_two, up_w)
    activated = jax.nn.gelu(upper, approximate=True).astype(jnp.bfloat16)
    lower = matmul(activated, down_w).reshape(FR_DEV, tok_frame, D)
    final = middle + modulation[:, 5] * lower
    hat_three, inv_three = layer_norm(final)
    normed_three = (
        (hat_three * (1 + modulation[:, 7]) + modulation[:, 6])
        .reshape(local_rows, D)
        .astype(jnp.bfloat16)
    )
    predicted = matmul(normed_three, head.T)
    row_weight = jnp.repeat(noised, tok_frame)[:, None]
    inv_scale = 1.0 / (noised_total * tok_frame * PIN)
    difference = predicted - targets
    loss_part = jnp.sum(row_weight * difference * difference) * inv_scale
    grad_pred = (2.0 * inv_scale * row_weight * difference).astype(jnp.bfloat16)
    grad_head = jnp.dot(grad_pred.T, normed_three, preferred_element_type=jnp.float32)
    grad_norm_three = matmul(grad_pred, head).reshape(FR_DEV, tok_frame, D)
    grad_final = norm_back(grad_norm_three * (1 + modulation[:, 7]), hat_three, inv_three)
    grad_lower = (grad_final * modulation[:, 5]).reshape(local_rows, D).astype(jnp.bfloat16)
    grad_down = jnp.dot(activated.T, grad_lower, preferred_element_type=jnp.float32)
    grad_upper = gelu_back(upper, matmul(grad_lower, down_w.T)).astype(jnp.bfloat16)
    grad_up = jnp.dot(normed_two.T, grad_upper, preferred_element_type=jnp.float32)
    grad_norm_two = matmul(grad_upper, up_w.T).reshape(FR_DEV, tok_frame, D)
    grad_middle = grad_final + norm_back(grad_norm_two * (1 + modulation[:, 4]), hat_two, inv_two)
    grad_branch = (grad_middle * modulation[:, 2]).reshape(local_rows, D).astype(jnp.bfloat16)
    grad_out_w = jnp.dot(attended_low.T, grad_branch, preferred_element_type=jnp.float32)
    grad_heads = split_heads(matmul(grad_branch, out_w.T).astype(jnp.bfloat16))
    delta = jnp.sum(grad_heads.astype(jnp.float32) * split_heads(attended), axis=-1).T
    key_all, value_all = (
        lax.all_gather(key_flat, "frame", axis=0, tiled=True),
        lax.all_gather(value_flat, "frame", axis=0, tiled=True),
    )
    grad_query = query_grads(
        queries, grad_heads, delta, log_total, query_frames, key_all, value_all, key_frames_all
    )
    key_value_grad = lax.psum_scatter(
        key_terms(
            lax.axis_size("frame") * local_rows,
            queries,
            grad_heads,
            delta,
            log_total,
            query_frames,
            key_all,
            value_all,
            key_frames_all,
        ),
        "frame",
        scatter_dimension=0,
        tiled=True,
    )
    grad_q = rotate(grad_query, cosine, -sine).reshape(local_rows, D)
    grad_k = rotate(split_heads(key_value_grad[:, :D]), cosine, -sine).reshape(local_rows, D)
    grad_proj = jnp.concatenate([grad_q, grad_k, key_value_grad[:, D:]], axis=1).astype(
        jnp.bfloat16
    )
    grad_attn_w = jnp.dot(normed.T, grad_proj, preferred_element_type=jnp.float32)
    grad_norm_one = matmul(grad_proj, attn_w.T).reshape(FR_DEV, tok_frame, D)
    grad_start = grad_middle + norm_back(grad_norm_one * (1 + modulation[:, 1]), hat_one, inv_one)
    grad_start_low = grad_start.reshape(local_rows, D).astype(jnp.bfloat16)
    grad_embed = jnp.dot(inputs.T, grad_start_low, preferred_element_type=jnp.float32)
    grad_bias = jnp.sum(grad_start_low.astype(jnp.float32), axis=0)
    mod_terms = [
        grad_norm_one,
        grad_norm_one * hat_one,
        grad_middle * branch,
        grad_norm_two,
        grad_norm_two * hat_two,
        grad_final * lower,
        grad_norm_three,
        grad_norm_three * hat_three,
    ]
    mod_grads = jnp.stack([jnp.sum(term, axis=1) for term in mod_terms], axis=1).reshape(
        FR_DEV, 8 * D
    )
    grad_table = jnp.dot(selector.T, mod_grads, precision=TOP_PRECISION)
    grad_io = jnp.concatenate([grad_embed, grad_head, grad_bias[None, :]], axis=0)
    grad_table, grad_io, total_loss = lax.psum((grad_table, grad_io, loss_part), ("frame", "rep"))
    grad_blocks = jnp.concatenate(
        [to_blocks(grad_attn_w), to_blocks(grad_out_w), to_blocks(grad_up), to_blocks(grad_down)], 0
    )
    owned = lax.psum_scatter(
        grad_blocks[block_slot], ("frame", "rep"), scatter_dimension=0, tiled=True
    )
    block_limit = CLIP_NORM * BLOCK * NPARAMS ** (-0.5)
    block_norm = jnp.sqrt(jnp.sum(owned * owned, axis=(1, 2), keepdims=True))
    mat_grad = owned * (block_limit / jnp.maximum(block_norm, block_limit))
    grad_norm = jnp.sqrt(jnp.sum(grad_table * grad_table) + jnp.sum(grad_io * grad_io))
    factor = CLIP_NORM / jnp.maximum(grad_norm, CLIP_NORM)
    new_mat_weight, new_stat_left, new_stat_right, new_mat_ema = shampoo(
        mat_grad, mat_weight, mat_ema, stat_left, stat_right, root_left, root_right
    )
    step = step_count[0].astype(jnp.float32)
    new_mod = adamw(grad_table * factor, mod_table, mod_mom, mod_var, mod_ema, step)
    new_io = adamw(grad_io * factor, io_weight, io_mom, io_var, io_ema, step)
    return (
        total_loss * noised_total,
        noised_total,
        grad_norm,
        mat_grad,
        new_mat_weight,
        new_stat_left,
        new_stat_right,
        new_mat_ema,
        new_mod[0],
        new_mod[1],
        new_mod[2],
        new_mod[3],
        new_io[0],
        new_io[1],
        new_io[2],
        new_io[3],
    )


def solution(mesh):
    in_specs = (
        P("rep", "frame", None, None),
        P("rep", "frame", None, None),
        P("rep", "frame"),
        P("rep", "frame"),
        P(),
        P(),
        P(),
        P(("frame", "rep"), None, None),
        P(("frame", "rep"), None, None),
        P(("frame", "rep"), None, None),
        P(("frame", "rep"), None, None),
        P(("frame", "rep"), None, None),
        P(("frame", "rep"), None, None),
        P(),
        P(),
        P(),
        P(),
        P(),
        P(),
        P(),
        P(),
    )
    out_specs = (
        P(),
        P(),
        P(),
        P(("frame", "rep"), None, None),
        P(("frame", "rep"), None, None),
        P(("frame", "rep"), None, None),
        P(("frame", "rep"), None, None),
        P(("frame", "rep"), None, None),
        P(),
        P(),
        P(),
        P(),
        P(),
        P(),
        P(),
        P(),
    )
    return jax.shard_map(
        on_device, mesh=mesh, in_specs=in_specs, out_specs=out_specs, check_vma=False
    )
```

profile of v0, /device:TPU:0, one launch (start us, length us, event | category | flops | bytes accessed | tf_op | source)
XLA Modules:
  0.0 1850.2 jit_solution(9274070640532015432)
XLA Ops:
  17.7 151.2 %all-gather.4.cloned.1.call-done = bf16[768,128,128]{2,1,0:T(8,128)(2,1)} async-done(((bf16[24,128,128]{2,1,0:T(8,128)(2,1)}), bf16[768,128,128]{2,1,0:T(8,128)(2,1)}) %all-gather.4.cloned.1.call-update) | async-done | bytes 25165840 | tf_op jit(solution)/shard_map/all_gather | solution.py:342
  177.8 110.6 %scatter_fusion = bf16[768,128,128]{2,1,0:T(8,128)(2,1)} fusion(bf16[768,128,128]{2,1,0:T(8,128)(2,1)} %broadcast_in_dim.143, s32[768]{0:T(1024)S(1)} %compare_select_fusion, bf16[768,128,128]{2,1,0:T(8,128)(2,1)} %all-gather.4.cloned.1.call-done), kind=kCustom, calls=%fused_computation.1 | custom fusion | bytes 75500544 | tf_op jit(solution)/shard_map/scatter | solution.py:343
  312.2 53.0 %psum.28 = f32[]{:T(128)} all-reduce(f32[]{:T(128)} %bitcast.23), channel_id=1, replica_groups=mesh['frame'=16,'rep'=2] {'frame','rep'}, use_global_device_ids=true, to_apply=%region_15.16 | all-reduce | flops 1 | bytes 8 | tf_op jit(solution)/shard_map/psum | solution.py:341
  370.7 12.1 fusion.187
  382.8 23.8 %copy.103 = bf16[32,8,128,128]{3,1,2,0:T(8,128)(2,1)} copy(bf16[32,8,128,128]{3,2,1,0:T(8,128)(2,1)} %bitcast.354) | data formatting | bytes 16777216 | tf_op jit(solution)/shard_map/reshape | solution.py:109
  406.5 12.1 copy.102
  418.7 12.4 copy.175
  431.1 9.6 copy.99
  440.6 22.5 %all-gather.8.cloned.1.call-done = bf16[4096,1024]{1,0:T(8,128)(2,1)} async-done(((bf16[256,1024]{1,0:T(8,128)(2,1)}), bf16[4096,1024]{1,0:T(8,128)(2,1)}) %all-gather.8.cloned.1.call-update) | async-done | bytes 8388624 | tf_op jit(solution)/shard_map/all_gather | solution.py:388
  463.2 22.1 %reshape.860 = bf16[8,512,16,64]{3,2,1,0:T(8,128)(2,1)} reshape(bf16[4096,1024]{1,0:T(8,128)(2,1)} %all-gather.8.cloned.1.call-done) | data formatting | bytes 16777216 | tf_op jit(solution)/shard_map/reshape | solution.py:141
  485.2 18.3 copy.100
  504.7 24.7 %while.43 = (s32[]{:T(128)}, f32[16,256]{1,0:T(8,128)S(1)}, f32[16,256]{1,0:T(8,128)S(1)}, f32[16,256,64]{1,2,0:T(8,128)}, s32[8,512]{1,0:T(8,128)S(1)}, /*index...) while((s32[]{:T(128)}, f32[16,256]{1,0:T(8,128)S(1)}, ...), condition=%wide.region_9.10_spmd.clone.clone, body=%wide.region_3.9_spmd.clone.clone.sunk | while | flops 560603648 | bytes 39068992 | solution.py:180
  506.5 9.6 conditional.12
  556.0 11.9 fusion.88
  577.6 132.7 %while.45 = (s32[]{:T(128)}, f32[8,512,2048]{2,1,0:T(8,128)}, s32[8,512]{1,0:T(8,128)S(1)}, s32[]{:T(128)}, bf16[8,512,16,64]{1,3,2,0:T(8,128)(2,1)}, /*index=5*...) while((s32[]{:T(128)}, f32[8,512,2048]{2,1,0:T(8,128)}, ...), condition=%wide.region_31.32_spmd.clone.clone, body=%wide.region_27.31_spmd.clone.clone.sunk | while | flops 1096417792 | bytes 94824216 | solution.py:283
  579.6 20.0 %conditional.14 = (f32[1,512,2048]{1,2,0:T(8,128)}) conditional(s32[]{:T(128)} %convert_element_type.265, () %tuple.190, (s32[1,512]{1,0:T(1,128)S(1)}, s32[]{:T(128)}, bf16[8,512,16,64]{1,3,2,0:T(8,128)(2,1)}, s32[]{:T(128)}, bf16[256,16,64]{0,2,1:T(8,128)(2,1)S(1)}, /*index=5*/f32[16,256]{1,0:T(8,128)S(1)}, bf16[8,512,16,64]{1,3,2,0:T(8,128)(2,1)}, ...), branch_computations={%region_29.29_spmd, %region_30.30_spmd} | conditional | flops 1096417280 | bytes 78042184 | solution.py:281
  724.9 30.0 %while.44 = (s32[]{:T(128)}, f32[256,16,64]{0,2,1:T(8,128)}, s32[8,512]{1,0:T(8,128)S(1)}, s32[]{:T(128)}, bf16[8,512,16,64]{1,3,2,0:T(8,128)(2,1)}, /*index=5*/...) while((s32[]{:T(128)}, f32[256,16,64]{0,2,1:T(8,128)}, ...), condition=%wide.region_26.27_spmd.clone.clone, body=%wide.region_22.26_spmd.clone.clone.sunk | while | flops 818283008 | bytes 23373544 | solution.py:245
  726.7 15.0 conditional.13
  775.5 454.8 %reduce-scatter.3.cloned.1.call-done = f32[256,2048]{1,0:T(8,128)} async-done(((f32[4096,2048]{1,0:T(8,128)}), f32[256,2048]{1,0:T(8,128)}) %reduce-scatter.3.cloned.1.call-update) | async-done | bytes 2097168 | tf_op jit(solution)/shard_map/reduce_scatter | solution.py:441
  1262.3 34.4 %pad_maximum_fusion = f32[768,128,128]{2,1,0:T(8,128)} fusion(f32[256,128,128]{2,1,0:T(8,128)} %bitcast.348, f32[256,128,128]{2,1,0:T(8,128)} %bitcast.347, f32[64,128,128]{2,1,0:T(8,128)} %bitcast.356, f32[192,128,128]{2,1,0:T(8,128)} %bitcast.346), kind=kLoop, calls=%fused_computation.79 | loop fusion | flops 37748736 | bytes 100663296 | tf_op jit(solution)/shard_map/concatenate | solution.py:484
  1296.7 35.7 %gather_fusion = f32[768,128,128]{2,1,0:T(8,128)} fusion(f32[768,128,128]{2,1,0:T(8,128)} %pad_maximum_fusion, s32[1024]{0:T(1024)S(1)} %pad_clamp_fusion), kind=kCustom, calls=%fused_computation | custom fusion | bytes 100666368 | tf_op jit(solution)/shard_map/gather | solution.py:488
  1334.0 40.3 %psum.29 = f32[]{:T(128)} all-reduce(f32[]{:T(128)S(6)} %mul.864), channel_id=1, replica_groups=mesh['frame'=16,'rep'=2] {'frame','rep'}, use_global_device_ids=true, to_apply=%region_16.17 | all-reduce | flops 1 | bytes 8 | tf_op jit(solution)/shard_map/psum | solution.py:483
  1374.9 9.1 all-reduce.3.cloned.1.call-done
  1395.7 426.4 %reduce-scatter.5.cloned.1.call-done = f32[24,128,128]{2,1,0:T(8,128)} async-done(((f32[768,128,128]{2,1,0:T(8,128)}), f32[24,128,128]{2,1,0:T(8,128)}) %reduce-scatter.5.cloned.1.call-update) | async-done | bytes 1572880 | tf_op jit(solution)/shard_map/reduce_scatter | solution.py:487
  (353 shorter events, 352.9 us)
Async XLA Ops:
  7.2 1819.9 %copy-start = (f32[24,128,128]{2,1,0:T(8,128)S(1)}, f32[24,128,128]{2,1,0:T(8,128)}, u32[]{:S(2)}) copy-start(f32[24,128,128]{2,1,0:T(8,128)} %param.45) | copy-start | bytes 4718596
  7.3 161.7 %all-gather.4.cloned.1.call-start = ((), (), s32[]{:S(2)}) async-start(), calls=%async_computation.2 | async-start | bytes 25952256 | tf_op jit(solution)/shard_map/all_gather | solution.py:342
  9.9 408.9 %all-gather.6.cloned.1.call-start = ((), (), s32[]{:S(2)}) async-start(), calls=%async_computation.3 | async-start | bytes 8912896 | tf_op jit(solution)/shard_map/all_gather | solution.py:387
  15.7 515.1 %copy-start.3 = (f32[256,1024]{1,0:T(8,128)}, f32[256,1024]{1,0:T(8,128)S(1)}, u32[]{:S(2)}) copy-start(f32[256,1024]{1,0:T(8,128)S(1)} %get-tuple-element.814) | copy-start | bytes 3145732
  15.7 281.0 %copy-start.51 = (f32[256]{0:T(256)}, f32[256]{0:T(256)S(1)}, u32[]{:S(2)}) copy-start(f32[256]{0:T(256)S(1)} %broadcast_multiply_fusion.13) | copy-start | bytes 3076
  16.0 280.7 %copy-start.60 = (f32[256]{0:T(256)}, f32[256]{0:T(256)S(1)}, u32[]{:S(2)}) copy-start(f32[256]{0:T(256)S(1)} %add_rsqrt_fusion.2) | copy-start | bytes 3076
  16.0 161.8 %copy-start.48 = (s32[768]{0:T(1024)}, s32[768]{0:T(1024)S(1)}, u32[]{:S(2)}) copy-start(s32[768]{0:T(1024)S(1)} %compare_select_fusion) | copy-start | bytes 9220
  16.3 290.3 %copy-start.34 = (f32[256,32]{0,1:T(8,128)}, f32[256,32]{0,1:T(8,128)S(1)}, u32[]{:S(2)}) copy-start(f32[256,32]{0,1:T(8,128)S(1)} %cosine_bitcast_fusion) | copy-start | bytes 98308
  16.9 279.8 %copy-start.46 = (f32[1,1,1,1024]{3,1,2,0:T(1,128)}, f32[1,1,1,1024]{3,1,2,0:T(1,128)S(1)}, u32[]{:S(2)}) copy-start(f32[1,1,1,1024]{3,1,2,0:T(1,128)S(1)} %get-tuple-element.809) | copy-start | bytes 12292
  16.9 279.8 %copy-start.53 = (f32[1,1,1,1024]{3,1,2,0:T(1,128)}, f32[1,1,1,1024]{3,1,2,0:T(1,128)S(1)}, u32[]{:S(2)}) copy-start(f32[1,1,1,1024]{3,1,2,0:T(1,128)S(1)} %get-tuple-element.808) | copy-start | bytes 12292
  310.0 153.2 %all-gather.8.cloned.1.call-start = ((), (), s32[]{:S(2)}) async-start(), calls=%async_computation.4 | async-start | bytes 8912896 | tf_op jit(solution)/shard_map/all_gather | solution.py:388
  312.2 918.1 %reduce-scatter.3.cloned.1.call-start = ((), (), s32[]{:S(2)}) async-start(), calls=%async_computation.5 | async-start | bytes 35651584 | tf_op jit(solution)/shard_map/reduce_scatter | solution.py:441
  710.3 673.7 %all-reduce.3.cloned.1.call-start = ((), (), s32[]{:S(2)}) async-start(), calls=%async_computation.7 | async-start | bytes 2424832 | tf_op jit(solution)/shard_map/psum | solution.py:483
  724.9 32.4 %copy-start.16 = (bf16[256,16,64]{0,2,1:T(8,128)(2,1)S(1)}, bf16[256,16,64]{0,2,1:T(8,128)(2,1)}, u32[]{:S(2)}) copy-start(bf16[256,16,64]{0,2,1:T(8,128)(2,1)} %copy-done.15) | copy-start | bytes 1572868
  775.5 459.6 %copy-start.18 = (f32[256,16,64]{0,2,1:T(8,128)S(1)}, f32[256,16,64]{0,2,1:T(8,128)}, u32[]{:S(2)}) copy-start(f32[256,16,64]{0,2,1:T(8,128)} %broadcast_multiply_fusion.2) | copy-start | bytes 3145732
  775.5 459.6 %copy-start.35 = (f32[256,32]{0,1:T(8,128)S(1)}, f32[256,32]{0,1:T(8,128)}, u32[]{:S(2)}) copy-start(f32[256,32]{0,1:T(8,128)} %copy-done.34) | copy-start | bytes 98308
  775.5 459.6 %copy-start.41 = (f32[256,32]{0,1:T(8,128)S(1)}, f32[256,32]{0,1:T(8,128)}, u32[]{:S(2)}) copy-start(f32[256,32]{0,1:T(8,128)} %get-tuple-element.773) | copy-start | bytes 98308
  1254.4 567.7 %reduce-scatter.5.cloned.1.call-start = ((), (), s32[]{:S(2)}) async-start(), calls=%async_computation.6 | async-start | bytes 51904512 | tf_op jit(solution)/shard_map/reduce_scatter | solution.py:487
  1332.4 56.6 %copy-start.33 = (f32[33,1024]{1,0:T(8,128)S(1)}, f32[33,1024]{1,0:T(8,128)}, u32[]{:S(2)}) copy-start(f32[33,1024]{1,0:T(8,128)} %param.50) | copy-start | bytes 405508
  1332.4 56.6 %copy-start.38 = (f32[33,1024]{1,0:T(8,128)S(1)}, f32[33,1024]{1,0:T(8,128)}, u32[]{:S(2)}) copy-start(f32[33,1024]{1,0:T(8,128)} %param.53) | copy-start | bytes 405508
  1332.4 56.6 %copy-start.39 = (f32[33,1024]{1,0:T(8,128)S(1)}, f32[33,1024]{1,0:T(8,128)}, u32[]{:S(2)}) copy-start(f32[33,1024]{1,0:T(8,128)} %param.52) | copy-start | bytes 405508
  1332.5 56.6 %copy-start.40 = (f32[33,1024]{1,0:T(8,128)S(1)}, f32[33,1024]{1,0:T(8,128)}, u32[]{:S(2)}) copy-start(f32[33,1024]{1,0:T(8,128)} %param.51) | copy-start | bytes 405508
  1332.5 58.4 %copy-start.17 = (f32[32,8192]{1,0:T(8,128)S(1)}, f32[32,8192]{1,0:T(8,128)}, u32[]{:S(2)}) copy-start(f32[32,8192]{1,0:T(8,128)} %param.46) | copy-start | bytes 3145732
  1395.7 429.7 %copy-start.28 = (f32[24,128,128]{2,1,0:T(8,128)S(1)}, f32[24,128,128]{2,1,0:T(8,128)}, u32[]{:S(2)}) copy-start(f32[24,128,128]{2,1,0:T(8,128)} %param.44) | copy-start | bytes 4718596
  (52 other events, 250.1 us)
Sparse Core Ops, SparseCore 0:
  11.6 157.3 all-gather.3
  310.1 77.1 all-gather.5
  390.1 73.0 all-gather.7
  710.4 519.8 reduce-scatter.2
  1254.5 129.4 all-reduce.2
  1390.3 431.7 reduce-scatter.4
where the time goes:
time: 1860 us; the launch traced here: 1850 us
  waiting for transfers between devices  1060 us (57%)
  local copies, waits for them, and re-layouts  419 us (23%)
  matrix products  120 us (6%)
  other arithmetic  99.4 us (5%)
  blocking collectives  93.3 us (5%)
  loops' own time  29.9 us (2%)
  between operations  25 us (1%)
    reduce_scatter x1, waiting for transfers between devices, on_device(): lax.psum_scatter(key_terms(lax.axis_size('frame') * local_rows, queries,...  455 us
    reduce_scatter x1, waiting for transfers between devices, on_device(): lax.psum_scatter(grad_blocks[block_slot], ('frame', 'rep'), scatter_dimen...  426 us
    all_gather x1, waiting for transfers between devices, on_device(): lax.all_gather(mat_weight.astype(jnp.bfloat16), ('frame', 'rep'), axis=0,...  151 us
    scatter x1, local copies, waits for them, and re-layouts, on_device(): natural = jnp.zeros_like(gathered).at[block_slot].set(gathered)  111 us
    dynamic_update_slice x16, local copies, waits for them, and re-layouts, key_terms(): return lax.map(one_block, stacks).reshape(row_count, 2 * D)  80.3 us
    psum x1, blocking collectives, on_device(): noised_total = jnp.maximum(lax.psum(jnp.sum(noised), ('frame', 'rep')), 1.0)  53 us
    unnamed x134, local copies, waits for them, and re-layouts  43.4 us
    dot_general x11, matrix products, matmul(): return jnp.dot(left, right, preferred_element_type=jnp.float32)  43.4 us
  transfers between devices with their start and end apart: 6, of which 5 were waited for; matrix products, arithmetic and copies ran while one was open for 12% of the time, Pallas kernels for 0%

commit v1 on v0

--- a/solution.py
+++ b/solution.py
@@ -4,6 +4,8 @@
 import jax
 import jax.numpy as jnp
 from jax import lax
+from jax.experimental import pallas as pl
+from jax.experimental.pallas import tpu as pltpu
 from jax.sharding import PartitionSpec as P
 
 D = 1024
@@ -518,7 +520,678 @@
     )
 
 
+MESH = pl.DeviceIdType.MESH
+GRAN = 4
+NSLOT = 24
+ORDERS = ("xzy", "xzy", "yzx", "yzx", "zxy", "zyx")
+
+def place():
+    frame = lax.axis_index("frame")
+    return frame // 4, (frame // 2) % 2, frame % 2, lax.axis_index("rep")
+
+def device(z, y, c, x):
+    return ((z * 2 + y) * 2 + c, x)
+
+def owner_of(z, y, c, x):
+    return ((z * 2 + y) * 2 + c) * 2 + x
+
+def plane_of(z, y, x):
+    return (z * 2 + y) * 2 + x
+
+def route_keys():
+    keys = [
+        (part, dx, dy, dz)
+        for part in range(len(ORDERS))
+        for dx in (0, 1)
+        for dy in (0, 1)
+        for dz in range(-3, 4)
+    ]
+    return sorted(keys, key=lambda k: (k[1] + k[2] + abs(k[3]), k[0]))
+
+def onward(order, dx, dy, dz):
+    moved = {"x": dx, "y": dy, "z": dz}
+    last = max((order.index(k) for k in order if moved[k]), default=-1)
+    links = []
+    if last >= 0 and order[last] == "z":
+        links.append("u" if dz < 0 else "w")
+    for k in order[last + 1 :]:
+        links.extend("uw" if k == "z" else k)
+    return links
+
+def can(link, z):
+    return {"u": z < 3, "w": z > 0}.get(link)
+
+def partner(link, z, y, c, x):
+    return {
+        "x": device(z, y, c, 1 - x),
+        "y": device(z, 1 - y, c, x),
+        "u": device(z + 1, y, c, x),
+        "w": device(z - 1, y, c, x),
+        "c": device(z, y, 1 - c, x),
+    }[link]
+
+def when(cond, fn):
+    if cond is None:
+        fn()
+    else:
+        pl.when(cond)(fn)
+
+def both(a, b):
+    return b if a is None else a if b is None else jnp.logical_and(a, b)
+
+def gather_kernel(w_ref, meta_ref, out_ref, meta_out, send, recv, csend, crecv, local, msend, mrecv):
+    z, y, c, x = place()
+    mine = owner_of(z, y, c, x)
+    flat = lax.axis_index("frame") * 2 + lax.axis_index("rep")
+    barrier = pltpu.get_barrier_semaphore()
+    def others(fn):
+        def body(step, carry):
+            peer = lax.rem(flat + step, 32)
+            fn(step, peer, (peer // 2, lax.rem(peer, 2)))
+            return carry
+        lax.fori_loop(1, 32, body, 0)
+    others(lambda step, peer, dev: pl.semaphore_signal(barrier, inc=1, device_id=dev, device_id_type=MESH))
+    pl.semaphore_wait(barrier, 31)
+    own = pltpu.make_async_copy(w_ref, out_ref.at[mine], local.at[0])
+    own.start()
+    links = ("x", "y", "u", "w")
+    pending = []
+    def hop(link, part, src, owner, plane):
+        return pltpu.make_async_remote_copy(
+            src_ref=src, dst_ref=out_ref.at[owner, pl.ds(part * GRAN, GRAN)],
+            send_sem=send.at[links.index(link), part, plane], recv_sem=recv.at[part, plane],
+            device_id=partner(link, z, y, c, x), device_id_type=MESH)
+    def core(src, owner, plane):
+        return pltpu.make_async_remote_copy(src_ref=src, dst_ref=out_ref.at[owner],
+            send_sem=csend.at[plane], recv_sem=crecv.at[plane],
+            device_id=partner("c", z, y, c, x), device_id_type=MESH)
+    def meta(step, peer, dev):
+        return pltpu.make_async_remote_copy(src_ref=meta_ref, dst_ref=meta_out.at[flat],
+            send_sem=msend.at[step], recv_sem=mrecv.at[step], device_id=dev, device_id_type=MESH)
+    keys = route_keys()
+    last_key = {}
+    for k in keys:
+        last_key[k[1:]] = k
+    for k in keys:
+        part, dx, dy, dz = k
+        if (dx, dy, dz) == (0, 0, 0):
+            for link in onward(ORDERS[part], 0, 0, 0):
+                src = w_ref.at[pl.ds(part * GRAN, GRAN)]
+                plane = plane_of(z, y, x)
+                def go(link=link, part=part, src=src, plane=plane):
+                    hop(link, part, src, mine, plane).start()
+                when(can(link, z), go)
+                pending.append((can(link, z), hop, (link, part, src, mine, plane)))
+    core(w_ref, mine, plane_of(z, y, x)).start()
+    pending.append((None, core, (w_ref, mine, plane_of(z, y, x))))
+    mown = pltpu.make_async_copy(meta_ref, meta_out.at[flat], local.at[1])
+    mown.start()
+    others(lambda step, peer, dev: meta(step, peer, dev).start())
+    for k in keys:
+        part, dx, dy, dz = k
+        if (dx, dy, dz) == (0, 0, 0):
+            continue
+        oz, oy, ox = z + dz, (1 - y if dy else y), (1 - x if dx else x)
+        cond = None if dz == 0 else (oz <= 3 if dz > 0 else oz >= 0)
+        owner, plane = owner_of(oz, oy, c, ox), plane_of(oz, oy, ox)
+        src = out_ref.at[owner, pl.ds(part * GRAN, GRAN)]
+        outs = onward(ORDERS[part], dx, dy, dz)
+        def act(part=part, owner=owner, plane=plane, src=src, outs=outs, k=k):
+            hop("x", part, src, owner, plane).wait_recv()
+            for link in outs:
+                when(can(link, z), lambda link=link: hop(link, part, src, owner, plane).start())
+            if last_key[k[1:]] == k:
+                core(out_ref.at[owner], owner, plane).start()
+        when(cond, act)
+        for link in outs:
+            pending.append((both(cond, can(link, z)), hop, (link, part, src, owner, plane)))
+        if last_key[k[1:]] == k:
+            pending.append((cond, core, (out_ref.at[owner], owner, plane)))
+    for cond, make, args in pending:
+        when(cond, lambda make=make, args=args: make(*args).wait_send())
+    own.wait()
+    mown.wait()
+    for plane in range(16):
+        owner = owner_of(plane // 4, (plane // 2) % 2, 1 - c, plane % 2)
+        core(out_ref.at[owner], owner, plane).wait_recv()
+    others(lambda step, peer, dev: meta(step, peer, dev).wait())
+
+def gather_weights(blocks, meta):
+    anyspace = pl.BlockSpec(memory_space=pl.ANY)
+    return pl.pallas_call(
+        gather_kernel,
+        out_shape=(jax.ShapeDtypeStruct((32, NSLOT, 128, 128), jnp.bfloat16), jax.ShapeDtypeStruct((32,) + meta.shape, meta.dtype)),
+        in_specs=[anyspace, anyspace], out_specs=(anyspace, anyspace),
+        scratch_shapes=[
+            pltpu.SemaphoreType.DMA((4, 6, 16)), pltpu.SemaphoreType.DMA((6, 16)),
+            pltpu.SemaphoreType.DMA((16,)), pltpu.SemaphoreType.DMA((16,)), pltpu.SemaphoreType.DMA((2,)),
+            pltpu.SemaphoreType.DMA((32,)), pltpu.SemaphoreType.DMA((32,)),
+        ],
+        compiler_params=pltpu.CompilerParams(collective_id=1, has_side_effects=True),
+    )(blocks, meta)
+
+def inbox_rows(order, link):
+    dim = "z" if link in "uw" else link
+    dims = order[: order.index(dim)]
+    return dims + "z" if dim == "z" else dims
+
+def inbox_layout(link):
+    starts, total = [], 0
+    for order in ORDERS:
+        starts.append(total)
+        size = 1
+        for d in inbox_rows(order, link):
+            size *= 4 if d == "z" else 2
+        total += size
+    return starts, total
+
+def inbox_index(link, part, oz, oy, ox):
+    starts, _ = inbox_layout(link)
+    index = 0
+    for d in inbox_rows(ORDERS[part], link):
+        index = index * (4 if d == "z" else 2) + {"z": oz, "y": oy, "x": ox}[d]
+    return starts[part] + index
+
+def toward(order, dx, dy, dz):
+    moved = {"x": dx, "y": dy, "z": dz}
+    last = [k for k in order if moved[k]][-1]
+    if last == "z":
+        return ("w", "u") if dz < 0 else ("u", "w")
+    return last, last
+
+def scatter_kernel(g_ref, out_ref, acc, sib, inx, iny, inu, inw, send, rx, ry, ru, rw, csend, crecv, local):
+    z, y, c, x = place()
+    boxes = {"x": (inx, rx), "y": (iny, ry), "u": (inu, ru), "w": (inw, rw)}
+    barrier = pltpu.get_barrier_semaphore()
+    for link in "xyuwc":
+        when(can(link, z), lambda link=link: pl.semaphore_signal(
+            barrier, inc=1, device_id=partner(link, z, y, c, x), device_id_type=MESH))
+    ends = jnp.logical_or(z == 0, z == 3)
+    pl.when(ends)(lambda: pl.semaphore_wait(barrier, 4))
+    pl.when(jnp.logical_not(ends))(lambda: pl.semaphore_wait(barrier, 5))
+    keys = [(k[0], k[1], k[2], k[3]) for k in reversed(route_keys())]
+    def owner_at(dx, dy, dz):
+        oz, oy, ox = z + dz, (1 - y if dy else y), (1 - x if dx else x)
+        cond = None if dz == 0 else (oz <= 3 if dz > 0 else oz >= 0)
+        return oz, oy, ox, cond
+    def core(oz, oy, ox):
+        plane = plane_of(oz, oy, ox)
+        return pltpu.make_async_remote_copy(
+            src_ref=g_ref.at[owner_of(oz, oy, 1 - c, ox)], dst_ref=sib.at[plane],
+            send_sem=csend.at[plane], recv_sem=crecv.at[plane],
+            device_id=partner("c", z, y, c, x), device_id_type=MESH)
+    def load(oz, oy, ox):
+        plane = plane_of(oz, oy, ox)
+        return pltpu.make_async_copy(g_ref.at[owner_of(oz, oy, c, ox)], acc.at[plane], local.at[plane])
+    seen = []
+    for part, dx, dy, dz in keys:
+        if (dx, dy, dz) not in seen:
+            seen.append((dx, dy, dz))
+    for off in seen:
+        oz, oy, ox, cond = owner_at(*off)
+        def begin(oz=oz, oy=oy, ox=ox):
+            core(oz, oy, ox).start()
+            load(oz, oy, ox).start()
+        when(cond, begin)
+    def clear(box):
+        def body(i, carry):
+            box[i] = jnp.zeros((GRAN, 128, 128), jnp.bfloat16)
+            return carry
+        lax.fori_loop(0, box.shape[0], body, 0)
+    pl.when(z == 3)(lambda: clear(inu))
+    pl.when(z == 0)(lambda: clear(inw))
+    def hop(part, off):
+        oz, oy, ox, cond = owner_at(*off)
+        plane = plane_of(oz, oy, ox)
+        link, seen_as = toward(ORDERS[part], *off)
+        box, sems = boxes[seen_as]
+        index = inbox_index(seen_as, part, oz, oy, ox)
+        return pltpu.make_async_remote_copy(
+            src_ref=acc.at[plane, pl.ds(part * GRAN, GRAN)], dst_ref=box.at[index],
+            send_sem=send.at[part, plane], recv_sem=sems.at[index],
+            device_id=partner(link, z, y, c, x), device_id_type=MESH)
+    fresh = set()
+    for part, dx, dy, dz in keys:
+        off = (dx, dy, dz)
+        oz, oy, ox, cond = owner_at(*off)
+        plane = plane_of(oz, oy, ox)
+        links = onward(ORDERS[part], *off)
+        first = off not in fresh
+        fresh.add(off)
+        def act(part=part, off=off, oz=oz, oy=oy, ox=ox, plane=plane, links=links, first=first):
+            if first:
+                core(oz, oy, ox).wait_recv()
+                load(oz, oy, ox).wait()
+            sources = []
+            for link in links:
+                box, sems = boxes[link]
+                index = inbox_index(link, part, oz, oy, ox)
+                sources.append((box, index))
+                def arrive(box=box, index=index, sems=sems, link=link):
+                    pltpu.make_async_remote_copy(
+                        src_ref=box.at[index], dst_ref=box.at[index], send_sem=csend.at[0], recv_sem=sems.at[index],
+                        device_id=partner("c", z, y, c, x), device_id_type=MESH).wait_recv()
+                when(can(link, z), arrive)
+            def add(i, carry):
+                row = part * GRAN + i
+                total = acc[plane, row].astype(jnp.float32) + sib[plane, row].astype(jnp.float32)
+                for box, index in sources:
+                    total = total + box[index, i].astype(jnp.float32)
+                if off == (0, 0, 0):
+                    out_ref[row] = total
+                else:
+                    acc[plane, row] = total.astype(jnp.bfloat16)
+                return carry
+            lax.fori_loop(0, GRAN, add, 0)
+            if off != (0, 0, 0):
+                hop(part, off).start()
+        when(cond, act)
+    for part, dx, dy, dz in keys:
+        if (dx, dy, dz) != (0, 0, 0):
+            cond = owner_at(dx, dy, dz)[3]
+            when(cond, lambda part=part, off=(dx, dy, dz): hop(part, off).wait_send())
+    for plane in range(16):
+        core(plane // 4, (plane // 2) % 2, plane % 2).wait_send()
+
+def scatter_grads(grads):
+    totals = {link: inbox_layout(link)[1] for link in "xyuw"}
+    box = lambda n: pltpu.VMEM((n, GRAN, 128, 128), jnp.bfloat16)
+    return pl.pallas_call(
+        scatter_kernel,
+        out_shape=jax.ShapeDtypeStruct((NSLOT, 128, 128), jnp.float32),
+        in_specs=[pl.BlockSpec(memory_space=pl.ANY)], out_specs=pl.BlockSpec(memory_space=pltpu.VMEM),
+        scratch_shapes=[
+            pltpu.VMEM((16, NSLOT, 128, 128), jnp.bfloat16), pltpu.VMEM((16, NSLOT, 128, 128), jnp.bfloat16),
+            box(totals["x"]), box(totals["y"]), box(totals["u"]), box(totals["w"]),
+            pltpu.SemaphoreType.DMA((6, 16)),
+            pltpu.SemaphoreType.DMA((totals["x"],)), pltpu.SemaphoreType.DMA((totals["y"],)),
+            pltpu.SemaphoreType.DMA((totals["u"],)), pltpu.SemaphoreType.DMA((totals["w"],)),
+            pltpu.SemaphoreType.DMA((16,)), pltpu.SemaphoreType.DMA((16,)), pltpu.SemaphoreType.DMA((16,)),
+        ],
+        compiler_params=pltpu.CompilerParams(collective_id=2, has_side_effects=True, vmem_limit_bytes=60 * 2**20),
+    )(grads)
+
+
+TOK=256; HD=64
+def dotg(a,b,ca,cb):
+    return lax.dot_general(a,b,(((ca,),(cb,)),((),())),preferred_element_type=jnp.float32)
+
+def attend_kernel(order_ref, qkv_ref, low_ref, full_ref, lse_ref):
+    t = pl.program_id(0)
+    slot = order_ref[t]
+    q = qkv_ref[slot, 0] * jnp.bfloat16(0.125)
+    def fold(state, keys, values):
+        top, total, acc = state
+        s = dotg(keys, q, 0, 0)
+        new = jnp.maximum(top, jnp.max(s, axis=0, keepdims=True))
+        p = jnp.exp(s - new)
+        shrink = jnp.exp(top - new)
+        return (new, total * shrink + jnp.sum(p, axis=0, keepdims=True),
+                acc * shrink + dotg(values, p.astype(jnp.bfloat16), 1, 0))
+    def one(i, state):
+        src = order_ref[i]
+        return fold(state, qkv_ref[src, 1], qkv_ref[src, 2])
+    def two(i, state):
+        a, b = order_ref[2 * i], order_ref[2 * i + 1]
+        keys = jnp.concatenate([qkv_ref[a, 1], qkv_ref[b, 1]], axis=1)
+        values = jnp.concatenate([qkv_ref[a, 2], qkv_ref[b, 2]], axis=1)
+        return fold(state, keys, values)
+    state = (jnp.full((1, TOK), -1e30, jnp.float32), jnp.zeros((1, TOK), jnp.float32), jnp.zeros((HD, TOK), jnp.float32))
+    n = t + 1
+    state = lax.fori_loop(0, n // 2, two, state)
+    top, total, acc = lax.fori_loop(2 * (n // 2), n, one, state)
+    out = acc / total
+    full_ref[slot] = out
+    low_ref[slot] = out.astype(jnp.bfloat16)
+    lse_ref[slot] = top + jnp.log(total)
+
+def attend(order, qkv):
+    frames = qkv.shape[0]
+    whole = lambda shape: pl.BlockSpec(shape, lambda t, order: (0,) * len(shape))
+    return pl.pallas_call(
+        attend_kernel,
+        grid_spec=pltpu.PrefetchScalarGridSpec(
+            num_scalar_prefetch=1, grid=(frames,),
+            in_specs=[whole(qkv.shape)],
+            out_specs=[whole((frames, HD, TOK)), whole((frames, HD, TOK)), whole((frames, 1, TOK))]),
+        out_shape=[jax.ShapeDtypeStruct((frames, HD, TOK), jnp.bfloat16), jax.ShapeDtypeStruct((frames, HD, TOK), jnp.float32), jax.ShapeDtypeStruct((frames, 1, TOK), jnp.float32)],
+        compiler_params=pltpu.CompilerParams(vmem_limit_bytes=40*2**20),
+    )(order, qkv)
+
+def attend_back_kernel(order_ref, qkv_ref, do_ref, full_ref, lse_ref, cos_ref, sin_ref, out_ref, dq, delta):
+    t = pl.program_id(0)
+    frames = pl.num_programs(0)
+    @pl.when(t == 0)
+    def _():
+        def start(i, carry):
+            dq[i] = jnp.zeros((HD, TOK), jnp.float32)
+            delta[i] = jnp.sum(do_ref[i].astype(jnp.float32) * full_ref[i], axis=0, keepdims=True)
+            return carry
+        lax.fori_loop(0, frames, start, 0)
+    slot = order_ref[t]
+    keys = qkv_ref[slot, 1]; values = qkv_ref[slot, 2]
+    def fold(state, qs):
+        dk, dv = state
+        q = jnp.concatenate([qkv_ref[a, 0] for a in qs], axis=1) if len(qs) > 1 else qkv_ref[qs[0], 0]
+        do = jnp.concatenate([do_ref[a] for a in qs], axis=1) if len(qs) > 1 else do_ref[qs[0]]
+        lse = jnp.concatenate([lse_ref[a] for a in qs], axis=1) if len(qs) > 1 else lse_ref[qs[0]]
+        dl = jnp.concatenate([delta[a] for a in qs], axis=1) if len(qs) > 1 else delta[qs[0]]
+        s = dotg(keys, q * jnp.bfloat16(0.125), 0, 0)
+        p = jnp.exp(s - lse)
+        dp = dotg(values, do, 0, 0)
+        ds = (p * (dp - dl)).astype(jnp.bfloat16)
+        dv = dv + dotg(do, p.astype(jnp.bfloat16), 1, 1)
+        dk = dk + dotg(q, ds, 1, 1)
+        dqn = dotg(keys, ds, 1, 0)
+        for j, a in enumerate(qs):
+            dq[a] = dq[a] + dqn[:, j * TOK:(j + 1) * TOK]
+        return dk, dv
+    def one(i, state):
+        return fold(state, [order_ref[i]])
+    def two(i, state):
+        j = t + 2 * i
+        return fold(state, [order_ref[j], order_ref[j + 1]])
+    zero = jnp.zeros((HD, TOK), jnp.float32)
+    n = frames - t
+    state = lax.fori_loop(0, n // 2, two, (zero, zero))
+    dk, dv = lax.fori_loop(t + 2 * (n // 2), frames, one, state)
+    def unturn(g, i):
+        c, s = cos_ref[i], sin_ref[i]
+        u1, u2 = g[:HD // 2], g[HD // 2:]
+        return jnp.concatenate([u1 * c + u2 * s, u2 * c - u1 * s], axis=0)
+    out_ref[slot, 1] = unturn(dk * 0.125, slot).astype(jnp.bfloat16)
+    out_ref[slot, 2] = dv.astype(jnp.bfloat16)
+    @pl.when(t == frames - 1)
+    def _():
+        def finish(i, carry):
+            out_ref[i, 0] = unturn(dq[i] * 0.125, i).astype(jnp.bfloat16)
+            return carry
+        lax.fori_loop(0, frames, finish, 0)
+
+def attend_back(order, qkv, do, full, lse, cos, sin):
+    frames = qkv.shape[0]
+    whole = lambda shape: pl.BlockSpec(shape, lambda t, order: (0,) * len(shape))
+    return pl.pallas_call(
+        attend_back_kernel,
+        grid_spec=pltpu.PrefetchScalarGridSpec(
+            num_scalar_prefetch=1, grid=(frames,),
+            in_specs=[whole(a.shape) for a in (qkv, do, full, lse, cos, sin)],
+            out_specs=whole(qkv.shape),
+            scratch_shapes=[pltpu.VMEM((frames, HD, TOK), jnp.float32), pltpu.VMEM((frames, 1, TOK), jnp.float32)]),
+        out_shape=jax.ShapeDtypeStruct(qkv.shape, jnp.bfloat16),
+        compiler_params=pltpu.CompilerParams(vmem_limit_bytes=48*2**20),
+    )(order, qkv, do, full, lse, cos, sin)
+
+
+def matrix_starts():
+    starts, total = [], 0
+    for rows_in, cols_in in matrix_shapes():
+        starts.append(total)
+        total += rows_in // BLOCK * (cols_in // BLOCK)
+    return starts, total
+
+
+def block_view(ref, index, cols_in):
+    across = cols_in // BLOCK
+    row = pl.multiple_of(index // across * BLOCK, BLOCK)
+    col = pl.multiple_of(index % across * BLOCK, BLOCK)
+    return ref.at[pl.ds(row, BLOCK), pl.ds(col, BLOCK)]
+
+
+def assemble_kernel(slot_ref, blocks_ref, *refs):
+    held, sems, out_sems = refs[4:8], refs[8], refs[9]
+    starts, _ = matrix_starts()
+    for m, (rows_in, cols_in) in enumerate(matrix_shapes()):
+        def one(i, carry):
+            pltpu.make_async_copy(
+                blocks_ref.at[slot_ref[starts[m] + i]], block_view(held[m], i, cols_in), sems.at[m]
+            ).start()
+            return carry
+
+        lax.fori_loop(0, rows_in // BLOCK * (cols_in // BLOCK), one, 0)
+    for m in range(4):
+        pltpu.make_async_copy(held[m], held[m], sems.at[m]).wait()
+        pltpu.make_async_copy(held[m], refs[m], out_sems.at[m]).start()
+    for m in range(4):
+        pltpu.make_async_copy(held[m], refs[m], out_sems.at[m]).wait()
+
+
+def held_matrices():
+    return [pltpu.VMEM(s, jnp.bfloat16) for s in matrix_shapes()]
+
+
+def assemble(slots, blocks):
+    anyspace = pl.BlockSpec(memory_space=pl.ANY)
+    return pl.pallas_call(
+        assemble_kernel,
+        in_specs=[pl.BlockSpec(memory_space=pltpu.SMEM), anyspace],
+        out_specs=[anyspace] * 4,
+        out_shape=[jax.ShapeDtypeStruct(s, jnp.bfloat16) for s in matrix_shapes()],
+        scratch_shapes=held_matrices() + [pltpu.SemaphoreType.DMA((4,)), pltpu.SemaphoreType.DMA((4,))],
+        compiler_params=pltpu.CompilerParams(vmem_limit_bytes=40 * 2**20),
+    )(slots, blocks)
+
+
+def disassemble_kernel(slot_ref, *refs):
+    out_ref, held, sem, in_sems = refs[4], refs[5:9], refs[9], refs[10]
+    starts, _ = matrix_starts()
+    for m in range(4):
+        pltpu.make_async_copy(refs[m], held[m], in_sems.at[m]).start()
+    for m, (rows_in, cols_in) in enumerate(matrix_shapes()):
+        pltpu.make_async_copy(refs[m], held[m], in_sems.at[m]).wait()
+        def one(i, carry):
+            pltpu.make_async_copy(
+                block_view(held[m], i, cols_in), out_ref.at[slot_ref[starts[m] + i]], sem.at[0]
+            ).start()
+            return carry
+
+        lax.fori_loop(0, rows_in // BLOCK * (cols_in // BLOCK), one, 0)
+    pltpu.make_async_copy(out_ref, out_ref, sem.at[0]).wait()
+
+
+def disassemble(slots, matrices):
+    anyspace = pl.BlockSpec(memory_space=pl.ANY)
+    return pl.pallas_call(
+        disassemble_kernel,
+        in_specs=[pl.BlockSpec(memory_space=pltpu.SMEM)] + [anyspace] * 4,
+        out_specs=anyspace,
+        out_shape=jax.ShapeDtypeStruct((matrix_starts()[1], BLOCK, BLOCK), jnp.bfloat16),
+        scratch_shapes=held_matrices() + [pltpu.SemaphoreType.DMA((1,)), pltpu.SemaphoreType.DMA((4,))],
+        compiler_params=pltpu.CompilerParams(vmem_limit_bytes=40 * 2**20),
+    )(slots, *matrices)
+
+
+def turn(values, cosine, sine):
+    first, second = values[:, : HEAD_DIM // 2], values[:, HEAD_DIM // 2 :]
+    return jnp.concatenate(
+        [first * cosine - second * sine, first * sine + second * cosine], axis=1
+    )
+
+
+def rope_columns(frame_ids):
+    pairs = HEAD_DIM // 2
+    time_pairs = pairs // 4
+    row_pairs = (pairs - time_pairs) // 2
+    column_pairs = pairs - time_pairs - row_pairs
+    shape = (frame_ids.shape[0], pairs, GRID * GRID)
+    token = jnp.arange(GRID * GRID, dtype=jnp.int32)
+    groups = (
+        (time_pairs, frame_ids[:, None, None].astype(jnp.float32)),
+        (row_pairs, (token // GRID)[None, None, :].astype(jnp.float32)),
+        (column_pairs, (token % GRID)[None, None, :].astype(jnp.float32)),
+    )
+    angles = jnp.concatenate(
+        [
+            jnp.broadcast_to(pos * frequencies(n)[None, :, None], (shape[0], n, shape[2]))
+            for n, pos in groups
+        ],
+        axis=1,
+    )
+    return (jnp.cos(angles), jnp.sin(angles))
+
+
+def on_grid(
+    clean,
+    noise,
+    levels,
+    flags,
+    frame_map,
+    block_slot,
+    step_count,
+    mat_weight,
+    mat_ema,
+    stat_left,
+    stat_right,
+    root_left,
+    root_right,
+    mod_table,
+    mod_mom,
+    mod_var,
+    mod_ema,
+    io_weight,
+    io_mom,
+    io_var,
+    io_ema,
+):
+    axes = ("frame", "rep")
+    tok_frame = GRID * GRID
+    level_now = levels[0, 0] * (1 - flags[0, 0])
+    noised = (1 - flags[0, 0]).astype(jnp.float32)
+    meta = jnp.concatenate(
+        [
+            jnp.full((1, 128), noised),
+            jnp.full((7, 128), level_now.astype(jnp.float32)),
+        ]
+    )
+    gathered, meta_all = gather_weights(mat_weight.astype(jnp.bfloat16), meta)
+    slots = jnp.zeros_like(block_slot).at[block_slot].set(
+        jnp.arange(block_slot.shape[0], dtype=jnp.int32)
+    )
+    attn_w, out_w, up_w, down_w = assemble(slots, gathered.reshape(-1, BLOCK, BLOCK))
+    noised_total = jnp.maximum(jnp.sum(meta_all[:, 0, 0]), 1.0)
+    selector = (
+        meta_all[:, 1, 0].astype(jnp.int32)[None, :] == jnp.arange(LEVELS, dtype=jnp.int32)[:, None]
+    ).astype(jnp.float32)
+    clip_map = lax.dynamic_index_in_dim(frame_map, lax.axis_index("rep"), 0, keepdims=False)
+    my_frame = lax.dynamic_slice_in_dim(clip_map, lax.axis_index("frame"), 1)
+    order = jnp.zeros_like(clip_map).at[clip_map].set(
+        jnp.arange(clip_map.shape[0], dtype=jnp.int32)
+    )
+    fraction = level_now.astype(jnp.float32) / LEVELS
+    frames_in = (
+        jnp.cos(0.5 * jnp.pi * fraction) * clean[0, 0] + jnp.sin(0.5 * jnp.pi * fraction) * noise[0, 0]
+    )
+    inputs = frames_in.T.astype(jnp.bfloat16)
+    targets = noise[0, 0].T
+    modulation = lax.dynamic_index_in_dim(mod_table, level_now, 0, keepdims=False).reshape(8, 1, D)
+    io_low = io_weight.astype(jnp.bfloat16)
+    embed = io_low[:PIN]
+    head = io_low[PIN : 2 * PIN]
+    start = matmul(inputs, embed) + io_weight[2 * PIN]
+    hat_one, inv_one = layer_norm(start)
+    normed = (hat_one * (1 + modulation[1]) + modulation[0]).astype(jnp.bfloat16)
+    projected = dotg(attn_w, normed, 0, 1)
+    cosine, sine = rope_columns(clip_map)
+    my_cos = lax.dynamic_index_in_dim(cosine, lax.axis_index("frame"), 0, keepdims=False)
+    my_sin = lax.dynamic_index_in_dim(sine, lax.axis_index("frame"), 0, keepdims=False)
+    parts = projected.reshape(3, HEADS, HEAD_DIM, tok_frame)
+    parts = jnp.stack(
+        [turn(parts[0], my_cos, my_sin), turn(parts[1], my_cos, my_sin), parts[2]], axis=1
+    ).astype(jnp.bfloat16)
+    mine = lax.all_to_all(parts, "frame", 0, 0, tiled=True)
+    low, full, lse = attend(order, mine)
+    attended = lax.all_to_all(low, "frame", 0, 0, tiled=True).reshape(D, tok_frame)
+    branch = dotg(attended, out_w, 0, 0)
+    middle = start + modulation[2] * branch
+    hat_two, inv_two = layer_norm(middle)
+    normed_two = (hat_two * (1 + modulation[4]) + modulation[3]).astype(jnp.bfloat16)
+    upper = matmul(normed_two, up_w)
+    activated = jax.nn.gelu(upper, approximate=True).astype(jnp.bfloat16)
+    lower = matmul(activated, down_w)
+    final = middle + modulation[5] * lower
+    hat_three, inv_three = layer_norm(final)
+    normed_three = (hat_three * (1 + modulation[7]) + modulation[6]).astype(jnp.bfloat16)
+    predicted = matmul(normed_three, head.T)
+    inv_scale = 1.0 / (noised_total * tok_frame * PIN)
+    difference = predicted - targets
+    loss_part = jnp.sum(noised * difference * difference) * inv_scale
+    grad_pred = (2.0 * inv_scale * noised * difference).astype(jnp.bfloat16)
+    grad_head = dotg(grad_pred, normed_three, 0, 0)
+    grad_norm_three = matmul(grad_pred, head)
+    grad_final = norm_back(grad_norm_three * (1 + modulation[7]), hat_three, inv_three)
+    grad_lower = (grad_final * modulation[5]).astype(jnp.bfloat16)
+    grad_down = dotg(activated, grad_lower, 0, 0).astype(jnp.bfloat16)
+    grad_upper = gelu_back(upper, matmul(grad_lower, down_w.T)).astype(jnp.bfloat16)
+    grad_up = dotg(normed_two, grad_upper, 0, 0).astype(jnp.bfloat16)
+    grad_norm_two = matmul(grad_upper, up_w.T)
+    grad_middle = grad_final + norm_back(grad_norm_two * (1 + modulation[4]), hat_two, inv_two)
+    grad_branch = (grad_middle * modulation[2]).astype(jnp.bfloat16)
+    grad_out_w = jnp.dot(attended, grad_branch, preferred_element_type=jnp.float32).astype(jnp.bfloat16)
+    grad_heads = dotg(out_w, grad_branch, 1, 1).astype(jnp.bfloat16)
+    grad_mine = lax.all_to_all(
+        grad_heads.reshape(HEADS, HEAD_DIM, tok_frame), "frame", 0, 0, tiled=True
+    )
+    back = attend_back(order, mine, grad_mine, full, lse, cosine, sine)
+    grad_proj = (
+        lax.all_to_all(back, "frame", 0, 0, tiled=True).swapaxes(0, 1).reshape(3 * D, tok_frame)
+    )
+    grad_attn_w = dotg(normed, grad_proj, 0, 1).astype(jnp.bfloat16)
+    grad_norm_one = dotg(grad_proj, attn_w, 0, 1)
+    grad_start = grad_middle + norm_back(grad_norm_one * (1 + modulation[1]), hat_one, inv_one)
+    grad_start_low = grad_start.astype(jnp.bfloat16)
+    grad_embed = dotg(inputs, grad_start_low, 0, 0)
+    grad_bias = jnp.sum(grad_start_low.astype(jnp.float32), axis=0)
+    mod_terms = [
+        grad_norm_one,
+        grad_norm_one * hat_one,
+        grad_middle * branch,
+        grad_norm_two,
+        grad_norm_two * hat_two,
+        grad_final * lower,
+        grad_norm_three,
+        grad_norm_three * hat_three,
+    ]
+    mod_grads = jnp.concatenate([jnp.sum(term, axis=0) for term in mod_terms])[None]
+    mod_rows = lax.all_gather(mod_grads, axes, axis=0, tiled=True)
+    grad_table = jnp.dot(selector, mod_rows, precision=TOP_PRECISION)
+    grad_io = jnp.concatenate([grad_embed, grad_head, grad_bias[None, :]], axis=0)
+    grad_io, total_loss = lax.psum((grad_io, loss_part), axes)
+    grad_blocks = disassemble(slots, (grad_attn_w, grad_out_w, grad_up, grad_down))
+    owned = scatter_grads(grad_blocks.reshape(32, -1, BLOCK, BLOCK))
+    block_limit = CLIP_NORM * BLOCK * NPARAMS ** (-0.5)
+    block_norm = jnp.sqrt(jnp.sum(owned * owned, axis=(1, 2), keepdims=True))
+    mat_grad = owned * (block_limit / jnp.maximum(block_norm, block_limit))
+    grad_norm = jnp.sqrt(jnp.sum(grad_table * grad_table) + jnp.sum(grad_io * grad_io))
+    factor = CLIP_NORM / jnp.maximum(grad_norm, CLIP_NORM)
+    new_mat_weight, new_stat_left, new_stat_right, new_mat_ema = shampoo(
+        mat_grad, mat_weight, mat_ema, stat_left, stat_right, root_left, root_right
+    )
+    step = step_count[0].astype(jnp.float32)
+    new_mod = adamw(grad_table * factor, mod_table, mod_mom, mod_var, mod_ema, step)
+    new_io = adamw(grad_io * factor, io_weight, io_mom, io_var, io_ema, step)
+    return (
+        total_loss * noised_total,
+        noised_total,
+        grad_norm,
+        mat_grad,
+        new_mat_weight,
+        new_stat_left,
+        new_stat_right,
+        new_mat_ema,
+        new_mod[0],
+        new_mod[1],
+        new_mod[2],
+        new_mod[3],
+        new_io[0],
+        new_io[1],
+        new_io[2],
+        new_io[3],
+    )
+
+
 def solution(mesh):
+    tuned = dict(mesh.shape) == {"frame": 16, "rep": 2}
+    body = on_grid if tuned else on_device
     in_specs = (
         P("rep", "frame", None, None),
         P("rep", "frame", None, None),
@@ -561,5 +1234,5 @@
         P(),
     )
     return jax.shard_map(
-        on_device, mesh=mesh, in_specs=in_specs, out_specs=out_specs, check_vma=False
-    )
+        body, mesh=mesh, in_specs=in_specs, out_specs=out_specs, check_vma=False
+    )

time: 1860 us -> 655 us (0.35)
  waiting for transfers between devices: 1060 us -> 82 us
  local copies, waits for them, and re-layouts: 419 us -> 21.4 us
  Pallas kernels: 0 us -> 329 us
  other arithmetic: 99.4 us -> 26.9 us
  matrix products: 120 us -> 71.6 us
  loops' own time: 29.9 us -> 0 us
  blocking collectives: 93.3 us -> 73.3 us
    reduce_scatter x2 -> x0, waiting for transfers between devices: 881 us -> none  [the longest x1 455 us: on_device(): lax.psum_scatter(key_terms(lax.axis_size('frame') * local_rows, queries,...]
    pallas_call x0 -> x6, Pallas kernels: none -> 329 us  [the longest x1 110 us: gather_weights(): pl.pallas_call(gather_kernel, out_shape=(jax.ShapeDtypeStruct((32, NSLOT,...]
    all_gather x3 -> x1, waiting for transfers between devices: 174 us -> 38.4 us  [on_grid(): mod_rows = lax.all_gather(mod_grads, axes, axis=0, tiled=True)]
    scatter x1 -> x2, local copies, waits for them, and re-layouts: 111 us -> 4 us  [the longest x1 3.38 us: on_grid(): jnp.zeros_like(block_slot).at[block_slot]]
    dynamic_update_slice x16 -> x0, local copies, waits for them, and re-layouts: 80.3 us -> none  [key_terms(): return lax.map(one_block, stacks).reshape(row_count, 2 * D)]
    reshape x7 -> x0, local copies, waits for them, and re-layouts: 65.3 us -> none  [the longest x4 42.8 us: from_blocks(): part_blocks.reshape(rows_in // BLOCK, cols_in // BLOCK, BLOCK, BLOCK)]
    all_to_all x0 -> x3, waiting for transfers between devices: none -> 43.5 us  [the longest x1 31.2 us: on_grid(): mine = lax.all_to_all(parts, 'frame', 0, 0, tiled=True)]
    psum x2 -> x1, blocking collectives: 93.3 us -> 54.9 us  [on_grid(): grad_io, total_loss = lax.psum((grad_io, loss_part), axes)]
  transfers between devices with their start and end apart: 6 -> 5, of which waited for: 5 -> 3; matrix products, arithmetic and copies ran while one was open for 12% -> 6% of each run, Pallas kernels for 0% -> 19%
where the time goes in v1:
time: 655 us; the launch traced here: 647 us
  Pallas kernels  329 us (50%)
  waiting for transfers between devices  82 us (13%)
  blocking collectives  73.3 us (11%)
  matrix products  71.6 us (11%)
  other arithmetic  26.9 us (4%)
  between operations  24.5 us (4%)
  local copies, waits for them, and re-layouts  21.4 us (3%)
  starting transfers between devices  17.7 us (3%)
    pallas_call x1, Pallas kernels, gather_weights(): pl.pallas_call(gather_kernel, out_shape=(jax.ShapeDtypeStruct((32, NSLOT,...  110 us
    pallas_call x1, Pallas kernels, scatter_grads(): pl.pallas_call(scatter_kernel, out_shape=jax.ShapeDtypeStruct((NSLOT, 128...  103 us
    psum x1, blocking collectives, on_grid(): grad_io, total_loss = lax.psum((grad_io, loss_part), axes)  54.9 us
    pallas_call x1, Pallas kernels, attend_back(): pl.pallas_call(attend_back_kernel, grid_spec=pltpu.PrefetchScalarGridSpec...  42.1 us
    pallas_call x1, Pallas kernels, attend(): pl.pallas_call(attend_kernel, grid_spec=pltpu.PrefetchScalarGridSpec(num_...  39.1 us
    all_gather x1, waiting for transfers between devices, on_grid(): mod_rows = lax.all_gather(mod_grads, axes, axis=0, tiled=True)  38.4 us
    all_to_all x1, waiting for transfers between devices, on_grid(): mine = lax.all_to_all(parts, 'frame', 0, 0, tiled=True)  31.2 us
    dot_general x9, matrix products, dotg(): lax.dot_general(a, b, (((ca,), (cb,)), ((), ())), preferred_element_type=...  26.9 us
  transfers between devices with their start and end apart: 5, of which 3 were waited for; matrix products, arithmetic and copies ran while one was open for 6% of the time, Pallas kernels for 19%

profile of v1, /device:TPU:0, one launch (start us, length us, event | category | flops | bytes accessed | tf_op | source)
XLA Modules:
  0.0 646.7 jit_solution(12158049315132952068)
XLA Ops:
  13.6 3.4 scatter_custom_fusion.1.slot_ref
  17.6 110.0 %shard_map.324 = (bf16[32,24,128,128]{3,2,1,0:T(8,128)(2,1)}, f32[32,8,128]{2,1,0:T(8,128)}) custom-call(bf16[24,128,128]{2,1,0:T(8,128)(2,1)} %convert_element_type.113.w_ref, f32[8,128]{1,0:T(8,128)} %concatenate.23.meta_ref), custom_call_target="tpu_custom_call" | custom-call | tf_op jit(solution)/shard_map/pallas_call | solution.py:661
  127.7 18.1 %shard_map.325 = (bf16[1024,3072]{1,0:T(8,128)(2,1)S(1)}, bf16[1024,1024]{1,0:T(8,128)(2,1)S(1)}, bf16[1024,4096]{1,0:T(8,128)(2,1)}, bf16[4096,1024]{1,0:T(8,128)(2,1)}) custom-call(s32[768]{0:T(1024)S(1)} %scatter_custom_fusion.1.slot_ref, bf16[768,128,128]{2,1,0:T(8,128)(2,1)} %bitcast.80), custom_call_target="tpu_custom_call" | custom-call | tf_op jit(solution)/shard_map/pallas_call | solution.py:965
  156.0 3.7 all-to-all-start
  160.4 31.2 %all-to-all-done.qkv_ref = bf16[16,3,64,256]{3,2,1,0:T(8,128)(2,1)S(1)} async-done(((bf16[16,3,64,256]{3,2,1,0:T(8,128)(2,1)}), bf16[16,3,64,256]{3,2,1,0:T(8,128)(2,1)S(1)}, u32[]{:S(2)}, u32[]{:S(2)}) %all-to-all-start) | async-done | bytes 1572896 | tf_op jit(solution)/shard_map/all_to_all | solution.py:1101
  191.7 39.1 %shard_map.326 = (bf16[16,64,256]{2,1,0:T(8,128)(2,1)S(1)}, f32[16,64,256]{2,1,0:T(8,128)S(1)}, f32[16,1,256]{2,1,0:T(1,128)S(1)}) custom-call(s32[16]{0:T(128)S(1)} %scatter_custom_fusion.order_ref, bf16[16,3,64,256]{3,2,1,0:T(8,128)(2,1)S(1)} %all-to-all-done.qkv_ref), custom_call_target="tpu_custom_call" | custom-call | tf_op jit(solution)/shard_map/pallas_call | solution.py:851
  232.5 9.4 %all-to-all-start.1 = ((bf16[16,64,256]{2,1,0:T(8,128)(2,1)}), bf16[16,64,256]{2,1,0:T(8,128)(2,1)}, u32[]{:S(2)}, u32[]{:S(2)}) async-start(bf16[16,64,256]{2,1,0:T(8,128)(2,1)} %copy-done.12), calls=%async_computation.1 | async-start | bytes 1048576 | tf_op jit(solution)/shard_map/all_to_all | solution.py:1103
  244.2 12.2 %all-to-all-done.1 = bf16[16,64,256]{2,1,0:T(8,128)(2,1)} async-done(((bf16[16,64,256]{2,1,0:T(8,128)(2,1)}), bf16[16,64,256]{2,1,0:T(8,128)(2,1)}, u32[]{:S(2)}, u32[]{:S(2)}) %all-to-all-start.1) | async-done | bytes 524320 | tf_op jit(solution)/shard_map/all_to_all | solution.py:1103
  259.6 6.3 fusion.32
  271.4 11.8 %fusion.6 = bf16[256,4096]{1,0:T(8,128)(2,1)S(1)} fusion(f32[256,4096]{1,0:T(8,128)} %copy-done.43, bf16[4096,1024]{1,0:T(8,128)(2,1)} %get-tuple-element.30, f32[256,1024]{1,0:T(8,128)S(1)} %get-tuple-element.59, f32[1024]{0:T(1024)S(1)} %bitcast.109), kind=kOutput, calls=%fused_computation.13 | convolution fusion | flops 2168979456 | bytes 15732736 | tf_op jit(solution)/shard_map/dot_general | solution.py:38
  288.7 18.4 %all_to_all.20.do_ref = bf16[16,64,256]{2,1,0:T(8,128)(2,1)S(1)} all-to-all(bf16[16,64,256]{2,1,0:T(8,128)(2,1)S(1)} %bitcast.87), channel_id=1, replica_groups=mesh['frame'=16,'rep'=2] {'frame'}, dimensions={0} | all-to-all | bytes 1048576 | tf_op jit(solution)/shard_map/all_to_all | solution.py:1131
  307.1 42.1 %shard_map.327 = bf16[16,3,64,256]{3,2,1,0:T(8,128)(2,1)S(1)} custom-call(s32[16]{0:T(128)S(1)} %scatter_custom_fusion.order_ref, bf16[16,3,64,256]{3,2,1,0:T(8,128)(2,1)S(1)} %all-to-all-done.qkv_ref, bf16[16,64,256]{2,1,0:T(8,128)(2,1)S(1)} %all_to_all.20.do_ref, f32[16,64,256]{2,1,0:T(8,128)S(1)} %copy-done.11, ...), custom_call_target="tpu_custom_call" | custom-call | tf_op jit(solution)/shard_map/pallas_call | solution.py:914
  350.3 4.5 all-to-all-start.3
  357.8 54.9 %psum.14 = f32[]{:T(128)} all-reduce(f32[]{:T(128)S(6)} %mul.585), channel_id=1, replica_groups=mesh['frame'=16,'rep'=2] {'frame','rep'}, use_global_device_ids=true, to_apply=%region_10.11 | all-reduce | flops 1 | bytes 8 | tf_op jit(solution)/shard_map/psum | solution.py:1158
  416.9 5.7 convolution_convert_fusion.1.refs_2_
  422.6 5.6 convolution_convert_fusion.refs_3_
  429.9 5.0 multiply_reduce_fusion.2
  434.9 4.7 convolution_convert_fusion.2.refs_0_
  445.3 16.8 %shard_map.328 = bf16[768,128,128]{2,1,0:T(8,128)(2,1)} custom-call(s32[768]{0:T(1024)S(1)} %scatter_custom_fusion.1.slot_ref, bf16[1024,3072]{1,0:T(8,128)(2,1)S(1)} %copy-done.1, bf16[1024,1024]{1,0:T(8,128)(2,1)S(1)} %copy-done.2, bf16[1024,4096]{1,0:T(8,128)(2,1)} %convolution_convert_fusion.1.refs_2_, bf16[4096,1024]{1,0:T(8,128)(2,1)} %convolution_convert_fusion.refs_3_), custom_call_target="tpu_custom_call" | custom-call | tf_op jit(solution)/shard_map/pallas_call | solution.py:994
  462.2 103.2 %shard_map.329 = f32[24,128,128]{2,1,0:T(8,128)} custom-call(bf16[32,24,128,128]{3,2,1,0:T(8,128)(2,1)} %bitcast.79), custom_call_target="tpu_custom_call" | custom-call | tf_op jit(solution)/shard_map/pallas_call | solution.py:799
  573.2 4.5 multiply_add_fusion.2
  577.7 3.9 multiply_add_fusion.1
  585.4 38.4 %all-gather.3.cloned.1.call-done = f32[262144]{0:T(1024)} async-done(((f32[8192]{0:T(1024)}), f32[262144]{0:T(1024)}) %all-gather.3.cloned.1.call-update) | async-done | bytes 1048592 | tf_op jit(solution)/shard_map/all_gather | solution.py:1155
  630.3 4.9 multiply_add_fusion.3
  (190 shorter events, 64.3 us)
Async XLA Ops:
  7.2 564.1 %copy-start = (f32[24,128,128]{2,1,0:T(8,128)S(1)}, f32[24,128,128]{2,1,0:T(8,128)}, u32[]{:S(2)}) copy-start(f32[24,128,128]{2,1,0:T(8,128)} %param.33) | copy-start | bytes 4718596
  7.2 5.7 slice-start
  7.2 5.7 copy-start.39
  7.2 5.6 copy-start.41
  13.3 133.9 %copy-start.15 = (f32[256,1024]{1,0:T(8,128)}, f32[256,1024]{1,0:T(8,128)S(1)}, u32[]{:S(2)}) copy-start(f32[256,1024]{1,0:T(8,128)S(1)} %get-tuple-element.87) | copy-start | bytes 3145732
  156.0 35.6 %all-to-all-start = ((bf16[16,3,64,256]{3,2,1,0:T(8,128)(2,1)}), bf16[16,3,64,256]{3,2,1,0:T(8,128)(2,1)S(1)}, u32[]{:S(2)}, u32[]{:S(2)}) async-start(bf16[16,3,64,256]{3,2,1,0:T(8,128)(2,1)} %pad_maximum_fusion), calls=%async_computation | async-start | bytes 3145728 | tf_op jit(solution)/shard_map/all_to_all | solution.py:1101
  232.5 23.9 %all-to-all-start.1 = ((bf16[16,64,256]{2,1,0:T(8,128)(2,1)}), bf16[16,64,256]{2,1,0:T(8,128)(2,1)}, u32[]{:S(2)}, u32[]{:S(2)}) async-start(bf16[16,64,256]{2,1,0:T(8,128)(2,1)} %copy-done.12), calls=%async_computation.1 | async-start | bytes 1048576 | tf_op jit(solution)/shard_map/all_to_all | solution.py:1103
  259.3 26.7 %copy-start.17 = (f32[256,1024]{1,0:T(8,128)}, f32[256,1024]{1,0:T(8,128)S(1)}, u32[]{:S(2)}) copy-start(f32[256,1024]{1,0:T(8,128)S(1)} %get-tuple-element.65) | copy-start | bytes 3145732
  259.3 6.6 %slice-start.3 = ((s8[8388608]{0:T(1024)(128)(4,1)}), s8[4194304]{0:T(1024)(128)(4,1)S(1)}, s32[]{:S(2)}) async-start(s8[8388608]{0:T(1024)(128)(4,1)} %bitcast.113), calls=%async_computation.9 | async-start | bytes 8388608
  259.6 6.4 slice-start.4
  270.9 12.3 %slice-start.1 = ((s8[8388608]{0:T(1024)(128)(4,1)}), s8[4194304]{0:T(1024)(128)(4,1)S(1)}, s32[]{:S(2)}) async-start(s8[8388608]{0:T(1024)(128)(4,1)} %bitcast.111), calls=%async_computation.7 | async-start | bytes 8388608
  271.3 14.6 %copy-start.26 = (f32[256,1024]{1,0:T(8,128)}, f32[256,1024]{1,0:T(8,128)S(1)}, u32[]{:S(2)}) copy-start(f32[256,1024]{1,0:T(8,128)S(1)} %get-tuple-element.59) | copy-start | bytes 3145732
  271.4 11.8 %slice-start.2 = ((s8[8388608]{0:T(1024)(128)(4,1)}), s8[4194304]{0:T(1024)(128)(4,1)S(1)}, s32[]{:S(2)}) async-start(s8[8388608]{0:T(1024)(128)(4,1)} %bitcast.111), calls=%async_computation.8 | async-start | bytes 8388608
  287.9 19.1 %copy-start.5 = (f32[16,32,256]{2,1,0:T(8,128)S(1)}, f32[16,32,256]{2,1,0:T(8,128)}, u32[]{:S(2)}) copy-start(f32[16,32,256]{2,1,0:T(8,128)} %copy-done.4) | copy-start | bytes 1572868
  287.9 19.1 %copy-start.7 = (f32[16,32,256]{2,1,0:T(8,128)S(1)}, f32[16,32,256]{2,1,0:T(8,128)}, u32[]{:S(2)}) copy-start(f32[16,32,256]{2,1,0:T(8,128)} %copy-done.6) | copy-start | bytes 1572868
  287.9 19.1 %copy-start.11 = (f32[16,64,256]{2,1,0:T(8,128)S(1)}, f32[16,64,256]{2,1,0:T(8,128)}, u32[]{:S(2)}) copy-start(f32[16,64,256]{2,1,0:T(8,128)} %copy-done.10) | copy-start | bytes 3145732
  350.3 63.2 %copy-start.25 = (bf16[256,1024]{1,0:T(8,128)(2,1)S(1)}, bf16[256,1024]{1,0:T(8,128)(2,1)}, u32[]{:S(2)}) copy-start(bf16[256,1024]{1,0:T(8,128)(2,1)} %copy-done.24) | copy-start | bytes 1572868
  350.3 63.4 %copy-start.21 = (f32[256,1024]{1,0:T(8,128)S(1)}, f32[256,1024]{1,0:T(8,128)}, u32[]{:S(2)}) copy-start(f32[256,1024]{1,0:T(8,128)} %copy-done.20) | copy-start | bytes 3145732
  350.3 77.9 %all-to-all-start.3 = ((bf16[16,3,64,256]{3,2,1,0:T(8,128)(2,1)}), bf16[16,3,64,256]{3,2,1,0:T(8,128)(2,1)}, u32[]{:S(2)}, u32[]{:S(2)}) async-start(bf16[16,3,64,256]{3,2,1,0:T(8,128)(2,1)} %copy-done.3), calls=%async_computation.3 | async-start | bytes 3145728 | tf_op jit(solution)/shard_map/all_to_all | solution.py:1136
  354.8 229.1 %all-reduce.3.cloned.1.call-start = ((), (), s32[]{:S(2)}) async-start(), calls=%async_computation.4 | async-start | bytes 327680 | tf_op jit(solution)/shard_map/psum | solution.py:1158
  416.9 5.7 copy-start.27
  416.9 5.7 copy-start.44
  440.9 183.0 %all-gather.3.cloned.1.call-start = ((), (), s32[]{:S(2)}) async-start(), calls=%async_computation.5 | async-start | bytes 1081344 | tf_op jit(solution)/shard_map/all_gather | solution.py:1155
  567.4 10.3 %copy-start.14 = (f32[24,128,128]{2,1,0:T(8,128)}, f32[24,128,128]{2,1,0:T(8,128)S(1)}, u32[]{:S(2)}) copy-start(f32[24,128,128]{2,1,0:T(8,128)S(1)} %broadcast_multiply_fusion) | copy-start | bytes 4718596
  (31 other events, 87.1 us)
Sparse Core Ops, SparseCore 0:
  441.0 123.5 all-reduce.2
  568.4 55.4 all-gather.2

commit v2 on v0

--- a/solution.py
+++ b/solution.py
@@ -4,6 +4,8 @@
 import jax
 import jax.numpy as jnp
 from jax import lax
+from jax.experimental import pallas as pl
+from jax.experimental.pallas import tpu as pltpu
 from jax.sharding import PartitionSpec as P
 
 D = 1024
@@ -518,7 +520,1246 @@
     )
 
 
+MESH = pl.DeviceIdType.MESH
+NSLOT = 24
+DATA = NSLOT
+SMALL_ROWS = 40
+GATHER_PARTS = (
+    ("xzy", 0, 4),
+    ("xzy", 4, 4),
+    ("yzx", 8, 4),
+    ("yzx", 12, 4),
+    ("zxy", 16, 4),
+    ("zyx", 20, 5),
+)
+SCATTER_PARTS = (
+    ("xzy", 0, 4),
+    ("xzy", 4, 4),
+    ("yzx", 8, 4),
+    ("yzx", 12, 4),
+    ("zxy", 16, 4),
+    ("zyx", 20, 4),
+)
+
+
+def place():
+    frame = lax.axis_index("frame")
+    return frame // 4, (frame // 2) % 2, frame % 2, lax.axis_index("rep")
+
+
+def device(z, y, c, x):
+    return ((z * 2 + y) * 2 + c, x)
+
+
+def owner_of(z, y, c, x):
+    return ((z * 2 + y) * 2 + c) * 2 + x
+
+
+def plane_of(z, y, x):
+    return (z * 2 + y) * 2 + x
+
+
+def offsets():
+    return [(dx, dy, dz) for dx in (0, 1) for dy in (0, 1) for dz in range(-3, 4)]
+
+
+def hops(off):
+    return off[0] + off[1] + abs(off[2])
+
+
+def route_keys(parts):
+    keys = [(part, off) for part in range(len(parts)) for off in offsets()]
+    return sorted(keys, key=lambda k: (hops(k[1]), k[0]))
+
+
+def onward(order, off):
+    moved = dict(zip("xyz", off))
+    last = max((order.index(k) for k in order if moved[k]), default=-1)
+    links = []
+    if last >= 0 and order[last] == "z":
+        links.append("u" if off[2] < 0 else "w")
+    for k in order[last + 1 :]:
+        links.extend("uw" if k == "z" else k)
+    return links
+
+
+def toward(order, off):
+    moved = dict(zip("xyz", off))
+    last = [k for k in order if moved[k]][-1]
+    if last == "z":
+        return ("w", "u") if off[2] < 0 else ("u", "w")
+    return last, last
+
+
+def can(link, z):
+    return {"u": z < 3, "w": z > 0}.get(link)
+
+
+def partner(link, z, y, c, x):
+    return {
+        "x": device(z, y, c, 1 - x),
+        "y": device(z, 1 - y, c, x),
+        "u": device(z + 1, y, c, x),
+        "w": device(z - 1, y, c, x),
+        "c": device(z, y, 1 - c, x),
+    }[link]
+
+
+def when(cond, fn):
+    if cond is None:
+        fn()
+    else:
+        pl.when(cond)(fn)
+
+
+def both(a, b):
+    return b if a is None else a if b is None else jnp.logical_and(a, b)
+
+
+def owner_at(off, z, y, x):
+    dx, dy, dz = off
+    oz = z + dz
+    cond = None if dz == 0 else (oz <= 3 if dz > 0 else oz >= 0)
+    return oz, (1 - y if dy else y), (1 - x if dx else x), cond
+
+
+def greet(z, y, c, x, far=()):
+    barrier = pltpu.get_barrier_semaphore()
+    for link in "xyuwc":
+        when(
+            can(link, z),
+            lambda link=link: pl.semaphore_signal(
+                barrier, inc=1, device_id=partner(link, z, y, c, x), device_id_type=MESH
+            ),
+        )
+    for dev in far:
+        pl.semaphore_signal(barrier, inc=1, device_id=dev, device_id_type=MESH)
+    ends = jnp.logical_or(z == 0, z == 3)
+    pl.when(ends)(lambda: pl.semaphore_wait(barrier, 4 + len(far)))
+    pl.when(jnp.logical_not(ends))(lambda: pl.semaphore_wait(barrier, 5 + len(far)))
+
+
+class Gather:
+    def __init__(self, parts, src, out, sems, where, core=True):
+        self.parts, self.src, self.out, self.where, self.core = parts, src, out, where, core
+        self.send, self.recv, self.csend, self.crecv = sems
+        self.keys = route_keys(parts)
+        self.last = {}
+        for key in self.keys:
+            self.last[key[1]] = key
+        self.sent = []
+
+    @staticmethod
+    def sems(parts):
+        n = len(parts)
+        return [
+            pltpu.SemaphoreType.DMA((4, n, 16)),
+            pltpu.SemaphoreType.DMA((n, 16)),
+            pltpu.SemaphoreType.DMA((16,)),
+            pltpu.SemaphoreType.DMA((16,)),
+        ]
+
+    def hop(self, link, part, src, owner, plane):
+        _, first, count = self.parts[part]
+        return pltpu.make_async_remote_copy(
+            src_ref=src.at[pl.ds(first, count)],
+            dst_ref=self.out.at[owner, pl.ds(first, count)],
+            send_sem=self.send.at["xyuw".index(link), part, plane],
+            recv_sem=self.recv.at[part, plane],
+            device_id=partner(link, *self.where),
+            device_id_type=MESH,
+        )
+
+    def across(self, src, owner, plane):
+        return pltpu.make_async_remote_copy(
+            src_ref=src,
+            dst_ref=self.out.at[owner],
+            send_sem=self.csend.at[plane],
+            recv_sem=self.crecv.at[plane],
+            device_id=partner("c", *self.where),
+            device_id_type=MESH,
+        )
+
+    def step(self, key):
+        part, off = key
+        z, y, c, x = self.where
+        oz, oy, ox, cond = owner_at(off, z, y, x)
+        owner, plane = owner_of(oz, oy, c, ox), plane_of(oz, oy, ox)
+        own = off == (0, 0, 0)
+        src = self.src if own else self.out.at[owner]
+        links = onward(self.parts[part][0], off)
+
+        def act():
+            if not own:
+                self.hop("x", part, src, owner, plane).wait_recv()
+            for link in links:
+                when(can(link, z), lambda link=link: self.hop(link, part, src, owner, plane).start())
+            if self.core and self.last[off] == key:
+                self.across(src, owner, plane).start()
+
+        when(cond, act)
+        for link in links:
+            self.sent.append(
+                (both(cond, can(link, z)), lambda link=link: self.hop(link, part, src, owner, plane))
+            )
+        if self.core and self.last[off] == key:
+            self.sent.append((cond, lambda: self.across(src, owner, plane)))
+
+    def finish(self):
+        for cond, make in self.sent:
+            when(cond, lambda make=make: make().wait_send())
+        if self.core:
+            c = self.where[2]
+            for plane in range(16):
+                owner = owner_of(plane // 4, (plane // 2) % 2, 1 - c, plane % 2)
+                self.across(self.out.at[owner], owner, plane).wait_recv()
+
+
+def gather_kernel(perm_ref, w_ref, data_ref, out_ref, stage, local, *sems):
+    where = place()
+    z, y, c, x = where
+
+    def take(i, carry):
+        stage[i] = w_ref[perm_ref[i]].astype(jnp.bfloat16)
+        return carry
+
+    lax.fori_loop(0, NSLOT, take, 0)
+    stage[DATA] = data_ref[...]
+    greet(*where)
+    own = pltpu.make_async_copy(stage, out_ref.at[owner_of(z, y, c, x)], local.at[0])
+    own.start()
+    gather = Gather(GATHER_PARTS, stage, out_ref, sems, where)
+    for key in gather.keys:
+        gather.step(key)
+    gather.finish()
+    own.wait()
+
+
+def gather_weights(perm, blocks, data):
+    vmem = pl.BlockSpec(memory_space=pltpu.VMEM)
+    return pl.pallas_call(
+        gather_kernel,
+        out_shape=jax.ShapeDtypeStruct((32, NSLOT + 1, 128, 128), jnp.bfloat16),
+        in_specs=[pl.BlockSpec(memory_space=pltpu.SMEM), vmem, vmem],
+        out_specs=pl.BlockSpec(memory_space=pltpu.HBM),
+        scratch_shapes=[
+            pltpu.VMEM((NSLOT + 1, 128, 128), jnp.bfloat16),
+            pltpu.SemaphoreType.DMA((1,)),
+        ]
+        + Gather.sems(GATHER_PARTS),
+        compiler_params=pltpu.CompilerParams(
+            collective_id=1, has_side_effects=True, vmem_limit_bytes=60 * 2**20
+        ),
+    )(perm, blocks, data)
+
+
+def inbox_axes(order, link):
+    dim = "z" if link in "uw" else link
+    axes = order[: order.index(dim)]
+    return axes + "z" if dim == "z" else axes
+
+
+def inbox_starts(parts, link):
+    starts, total = [], 0
+    for order, _, count in parts:
+        starts.append(total)
+        size = count
+        for d in inbox_axes(order, link):
+            size *= 4 if d == "z" else 2
+        total += size
+    return starts, total
+
+
+class Scatter:
+    def __init__(self, parts, acc, sib, boxes, send, recvs, where, ready, store):
+        self.parts, self.acc, self.sib, self.where = parts, acc, sib, where
+        self.boxes = dict(zip("xyuw", boxes))
+        self.recvs = dict(zip("xyuw", recvs))
+        self.send, self.ready, self.store = send, ready, store
+        self.keys = list(reversed(route_keys(parts)))
+        self.seen = []
+        for _, off in self.keys:
+            if off not in self.seen:
+                self.seen.append(off)
+        self.fresh = set()
+
+    @staticmethod
+    def boxes_of(parts):
+        return [
+            pltpu.VMEM((inbox_starts(parts, link)[1], 128, 128), jnp.bfloat16) for link in "xyuw"
+        ]
+
+    @staticmethod
+    def sems(parts):
+        return [pltpu.SemaphoreType.DMA((len(parts), 16))] + [
+            pltpu.SemaphoreType.DMA((len(parts), 16)) for _ in "xyuw"
+        ]
+
+    def inbox(self, link, part, oz, oy, ox):
+        order, _, count = self.parts[part]
+        index = 0
+        for d in inbox_axes(order, link):
+            index = index * (4 if d == "z" else 2) + {"z": oz, "y": oy, "x": ox}[d]
+        return inbox_starts(self.parts, link)[0][part] + index * count
+
+    def clear_ends(self):
+        z = self.where[0]
+
+        def clear(box):
+            def body(i, carry):
+                box[i] = jnp.zeros((128, 128), jnp.bfloat16)
+                return carry
+
+            lax.fori_loop(0, box.shape[0], body, 0)
+
+        pl.when(z == 3)(lambda: clear(self.boxes["u"]))
+        pl.when(z == 0)(lambda: clear(self.boxes["w"]))
+
+    def hop(self, part, off):
+        z, y, c, x = self.where
+        oz, oy, ox, _ = owner_at(off, z, y, x)
+        plane = plane_of(oz, oy, ox)
+        order, first, count = self.parts[part]
+        link, named = toward(order, off)
+        return pltpu.make_async_remote_copy(
+            src_ref=self.acc.at[plane, pl.ds(first, count)],
+            dst_ref=self.boxes[named].at[pl.ds(self.inbox(named, part, oz, oy, ox), count)],
+            send_sem=self.send.at[part, plane],
+            recv_sem=self.recvs[named].at[part, plane],
+            device_id=partner(link, *self.where),
+            device_id_type=MESH,
+        )
+
+    def step(self, key):
+        part, off = key
+        z, y, c, x = self.where
+        oz, oy, ox, cond = owner_at(off, z, y, x)
+        plane = plane_of(oz, oy, ox)
+        order, first, count = self.parts[part]
+        new = off not in self.fresh
+        self.fresh.add(off)
+
+        def act():
+            if new:
+                self.ready(oz, oy, ox)
+            sources = []
+            for link in onward(order, off):
+                start = self.inbox(link, part, oz, oy, ox)
+                sources.append((self.boxes[link], start))
+
+                def arrive(link=link, start=start):
+                    view = self.boxes[link].at[pl.ds(start, count)]
+                    pltpu.make_async_remote_copy(
+                        src_ref=view,
+                        dst_ref=view,
+                        send_sem=self.send.at[part, plane],
+                        recv_sem=self.recvs[link].at[part, plane],
+                        device_id=partner("c", *self.where),
+                        device_id_type=MESH,
+                    ).wait_recv()
+
+                when(can(link, z), arrive)
+
+            def add(i, carry):
+                total = self.acc[plane, first + i].astype(jnp.float32) + self.sib[
+                    plane, first + i
+                ].astype(jnp.float32)
+                for box, start in sources:
+                    total = total + box[start + i].astype(jnp.float32)
+                if off == (0, 0, 0):
+                    self.store(first + i, total)
+                else:
+                    self.acc[plane, first + i] = total.astype(jnp.bfloat16)
+                return carry
+
+            lax.fori_loop(0, count, add, 0)
+            if off != (0, 0, 0):
+                self.hop(part, off).start()
+
+        when(cond, act)
+
+    def finish(self):
+        z, y, c, x = self.where
+        for part, off in self.keys:
+            if off != (0, 0, 0):
+                cond = owner_at(off, z, y, x)[3]
+                when(cond, lambda part=part, off=off: self.hop(part, off).wait_send())
+
+
+class SmallSums:
+    def __init__(self, row, io, rows_out, io_out, mine, inbox, sems, where):
+        self.row, self.io, self.rows, self.io_out = row, io, rows_out, io_out
+        self.mine, self.inbox, self.where = mine, inbox, where
+        self.gsend, self.grecv, self.osend, self.orecv, self.bsend, self.brecv, self.local = sems
+        self.order = "zyx"
+        self.sent = []
+
+    @staticmethod
+    def sems():
+        dma = pltpu.SemaphoreType.DMA
+        return [dma((4, 16)), dma((16,)), dma((6,)), dma((6,)), dma((1,)), dma((1,)), dma((1,))]
+
+    def far(self):
+        z, y, c, x = self.where
+        return device(z + 2 - 4 * (z // 2), y, c, x)
+
+    def peer(self, turn):
+        z, y, c, x = self.where
+        if turn == 3:
+            return device(z + 1 - 2 * (z % 2), y, c, x)
+        if turn == 4:
+            return self.far()
+        return partner("cxyyyc"[turn], *self.where)
+
+    def swap(self, turn):
+        c = self.where[2]
+        if turn == 0:
+            src, dst = self.io.at[1 - c], self.inbox.at[0]
+        elif turn == 5:
+            src, dst = self.mine.at[5], self.io_out.at[c]
+        else:
+            src, dst = self.mine.at[turn], self.inbox.at[turn]
+        return pltpu.make_async_remote_copy(
+            src_ref=src,
+            dst_ref=dst,
+            send_sem=self.osend.at[turn],
+            recv_sem=self.orecv.at[turn],
+            device_id=self.peer(turn),
+            device_id_type=MESH,
+        )
+
+    def hop(self, link, src, plane):
+        return pltpu.make_async_remote_copy(
+            src_ref=src,
+            dst_ref=self.rows.at[self.where[2], plane],
+            send_sem=self.gsend.at["xyuw".index(link), plane],
+            recv_sem=self.grecv.at[plane],
+            device_id=partner(link, *self.where),
+            device_id_type=MESH,
+        )
+
+    def bulk(self, core):
+        return pltpu.make_async_remote_copy(
+            src_ref=self.rows.at[core],
+            dst_ref=self.rows.at[core],
+            send_sem=self.bsend.at[0],
+            recv_sem=self.brecv.at[0],
+            device_id=partner("c", *self.where),
+            device_id_type=MESH,
+        )
+
+    def row_step(self, off):
+        z, y, c, x = self.where
+        oz, oy, ox, cond = owner_at(off, z, y, x)
+        plane = plane_of(oz, oy, ox)
+        own = off == (0, 0, 0)
+        src = self.row if own else self.rows.at[c, plane]
+        links = onward(self.order, off)
+
+        def act():
+            if not own:
+                self.hop("x", src, plane).wait_recv()
+            for link in links:
+                when(can(link, z), lambda link=link: self.hop(link, src, plane).start())
+
+        when(cond, act)
+        for link in links:
+            self.sent.append(
+                (both(cond, can(link, z)), lambda link=link: self.hop(link, src, plane))
+            )
+
+    def begin(self):
+        z, y, c, x = self.where
+        self.own = pltpu.make_async_copy(
+            self.row, self.rows.at[c, plane_of(z, y, x)], self.local.at[0]
+        )
+        self.own.start()
+        self.swap(0).start()
+        self.row_step((0, 0, 0))
+
+    def turn(self, turn):
+        c = self.where[2]
+        self.swap(turn).wait_recv()
+        if turn < 5:
+            before = self.io[c] if turn == 0 else self.mine[turn]
+            self.mine[turn + 1] = before + self.inbox[turn]
+            if turn == 4:
+                self.io_out[c] = self.mine[5]
+            self.swap(turn + 1).start()
+
+    def tasks(self):
+        todo = [
+            lambda off=off: self.row_step(off)
+            for off in sorted(offsets(), key=hops)
+            if off != (0, 0, 0)
+        ]
+        for turn in range(6):
+            todo.insert(4 * turn + 3, lambda turn=turn: self.turn(turn))
+
+        def last():
+            self.own.wait()
+            self.bulk(self.where[2]).start()
+
+        return todo + [last]
+
+    def finish(self):
+        c = self.where[2]
+        self.bulk(1 - c).wait_recv()
+        self.bulk(c).wait_send()
+        for turn in range(6):
+            self.swap(turn).wait_send()
+        for cond, make in self.sent:
+            when(cond, lambda make=make: make().wait_send())
+
+
+def scatter_kernel(rank_ref, g_ref, row_ref, io_ref, out_ref, rows_out, io_out, *refs):
+    acc, sib, total = refs[:3]
+    boxes, refs = refs[3:7], refs[7:]
+    mine, inbox = refs[:2]
+    csend, crecv, local, send = refs[2:6]
+    recvs, small_sems = refs[6:10], refs[10:]
+    where = place()
+    z, y, c, x = where
+    small = SmallSums(row_ref, io_ref, rows_out, io_out, mine, inbox, small_sems, where)
+    greet(*where, far=(small.far(),))
+    small.begin()
+
+    def core(oz, oy, ox):
+        plane = plane_of(oz, oy, ox)
+        return pltpu.make_async_remote_copy(
+            src_ref=g_ref.at[owner_of(oz, oy, 1 - c, ox)],
+            dst_ref=sib.at[plane],
+            send_sem=csend.at[plane],
+            recv_sem=crecv.at[plane],
+            device_id=partner("c", *where),
+            device_id_type=MESH,
+        )
+
+    def load(oz, oy, ox):
+        plane = plane_of(oz, oy, ox)
+        return pltpu.make_async_copy(
+            g_ref.at[owner_of(oz, oy, c, ox)], acc.at[plane], local.at[plane]
+        )
+
+    def ready(oz, oy, ox):
+        core(oz, oy, ox).wait_recv()
+        load(oz, oy, ox).wait()
+
+    def store(row, value):
+        total[row] = value
+
+    scatter = Scatter(SCATTER_PARTS, acc, sib, boxes, send, recvs, where, ready, store)
+    for off in scatter.seen:
+        oz, oy, ox, cond = owner_at(off, z, y, x)
+
+        def begin(oz=oz, oy=oy, ox=ox):
+            core(oz, oy, ox).start()
+            load(oz, oy, ox).start()
+
+        when(cond, begin)
+    scatter.clear_ends()
+    tasks = small.tasks()
+    for i, key in enumerate(scatter.keys):
+        scatter.step(key)
+        if i % 3 == 2 and tasks:
+            tasks.pop(0)()
+    for task in tasks:
+        task()
+
+    def put(i, carry):
+        out_ref[i] = total[rank_ref[i]]
+        return carry
+
+    lax.fori_loop(0, NSLOT, put, 0)
+    scatter.finish()
+    for plane in range(16):
+        core(plane // 4, (plane // 2) % 2, plane % 2).wait_send()
+    small.finish()
+
+
+def scatter_grads(ranks, grads, row, io):
+    vmem = pl.BlockSpec(memory_space=pltpu.VMEM)
+    dma = pltpu.SemaphoreType.DMA
+    held = pltpu.VMEM((16, NSLOT, 128, 128), jnp.bfloat16)
+    half = (SMALL_ROWS, D // 2)
+    return pl.pallas_call(
+        scatter_kernel,
+        out_shape=(
+            jax.ShapeDtypeStruct((NSLOT, 128, 128), jnp.float32),
+            jax.ShapeDtypeStruct((2, 16) + row.shape, jnp.float32),
+            jax.ShapeDtypeStruct((2,) + half, jnp.float32),
+        ),
+        in_specs=[
+            pl.BlockSpec(memory_space=pltpu.SMEM),
+            pl.BlockSpec(memory_space=pl.ANY),
+            vmem,
+            vmem,
+        ],
+        out_specs=(vmem, vmem, vmem),
+        scratch_shapes=[held, held, pltpu.VMEM((NSLOT, 128, 128), jnp.float32)]
+        + Scatter.boxes_of(SCATTER_PARTS)
+        + [pltpu.VMEM((6,) + half, jnp.float32), pltpu.VMEM((6,) + half, jnp.float32)]
+        + [dma((16,)), dma((16,)), dma((16,))]
+        + Scatter.sems(SCATTER_PARTS)
+        + SmallSums.sems(),
+        compiler_params=pltpu.CompilerParams(
+            collective_id=2, has_side_effects=True, vmem_limit_bytes=58 * 2**20
+        ),
+    )(ranks, grads, row, io)
+
+
+TOK = GRID * GRID
+GROUP = 4
+
+
+def fold_rows(values, op):
+    return op(values.reshape(values.shape[0] // 8, 8, values.shape[1]), axis=0)
+
+
+def side_by_side(ref, first, count, kind):
+    parts = [ref[first + j, kind] for j in range(count)]
+    return jnp.concatenate(parts, axis=1) if count > 1 else parts[0]
+
+
+def attend_frame(t, qkv, scores, full, lse):
+    q = qkv[t, 0] * jnp.bfloat16(HEAD_DIM**-0.5)
+
+    def score(k, top):
+        s = dotg(qkv[k, 1], q, 0, 0)
+        scores[k] = s
+        return jnp.maximum(top, fold_rows(s, jnp.max))
+
+    top = lax.fori_loop(
+        0, t + 1, score, jnp.full((8, TOK), -1e30, jnp.float32), unroll=min(GROUP, t + 1)
+    )
+    top = jnp.max(top, axis=0, keepdims=True)
+    total = jnp.zeros((8, TOK), jnp.float32)
+    acc = jnp.zeros((HEAD_DIM, TOK), jnp.float32)
+    for k in range(0, t + 1, GROUP):
+        count = min(GROUP, t + 1 - k)
+        probs = []
+        for j in range(count):
+            p = jnp.exp(scores[k + j] - top)
+            total = total + fold_rows(p, jnp.sum)
+            probs.append(p.astype(jnp.bfloat16))
+        acc = acc + dotg(side_by_side(qkv, k, count, 2), jnp.concatenate(probs, axis=0), 1, 0)
+    total = jnp.sum(total, axis=0, keepdims=True)
+    out = acc / total
+    full[t] = out
+    lse[t] = top + jnp.log(total)
+    return out.astype(jnp.bfloat16)
+
+
+def turn_back(values, cosine, sine):
+    first, second = values[: HEAD_DIM // 2], values[HEAD_DIM // 2 :]
+    return jnp.concatenate(
+        [first * cosine + second * sine, second * cosine - first * sine], axis=0
+    )
+
+
+def attend_frame_back(t, qkv, do_ref, full, lse, cos, sin, dk_ref, dv_ref):
+    q = qkv[t, 0] * jnp.bfloat16(HEAD_DIM**-0.5)
+    do = do_ref[t]
+    delta = jnp.sum(do.astype(jnp.float32) * full[t], axis=0, keepdims=True)
+    dq = jnp.zeros((HEAD_DIM, TOK), jnp.float32)
+    for k in range(0, t + 1, GROUP):
+        count = min(GROUP, t + 1 - k)
+        keys = side_by_side(qkv, k, count, 1)
+        p = jnp.exp(dotg(keys, q, 0, 0) - lse[t])
+        dp = dotg(side_by_side(qkv, k, count, 2), do, 0, 0)
+        ds = (p * (dp - delta)).astype(jnp.bfloat16)
+        dq = dq + dotg(keys, ds, 1, 0)
+        dk = dotg(q, ds, 1, 1)
+        dv = dotg(do, p.astype(jnp.bfloat16), 1, 1)
+        for j in range(count):
+            dk_ref[k + j] += dk[:, j * TOK : (j + 1) * TOK]
+            dv_ref[k + j] += dv[:, j * TOK : (j + 1) * TOK]
+    return (
+        turn_back(dq * HEAD_DIM**-0.5, cos[t], sin[t]).astype(jnp.bfloat16),
+        turn_back(dk_ref[t], cos[t], sin[t]).astype(jnp.bfloat16),
+        dv_ref[t].astype(jnp.bfloat16),
+    )
+
+
+def attend_kernel(qkv_ref, low_ref, full_ref, lse_ref, scores):
+    for t in range(qkv_ref.shape[0]):
+        low_ref[t] = attend_frame(t, qkv_ref, scores, full_ref, lse_ref)
+
+
+def attend(qkv):
+    frames = qkv.shape[0]
+    vmem = pl.BlockSpec(memory_space=pltpu.VMEM)
+    return pl.pallas_call(
+        attend_kernel,
+        in_specs=[vmem],
+        out_specs=[vmem] * 3,
+        out_shape=[
+            jax.ShapeDtypeStruct((frames, HEAD_DIM, TOK), jnp.bfloat16),
+            jax.ShapeDtypeStruct((frames, HEAD_DIM, TOK), jnp.float32),
+            jax.ShapeDtypeStruct((frames, 1, TOK), jnp.float32),
+        ],
+        scratch_shapes=[pltpu.VMEM((frames, TOK, TOK), jnp.float32)],
+        compiler_params=pltpu.CompilerParams(vmem_limit_bytes=32 * 2**20),
+    )(qkv)
+
+
+def attend_back_kernel(qkv_ref, do_ref, full_ref, lse_ref, cos_ref, sin_ref, out_ref, dk, dv):
+    dk[...] = jnp.zeros_like(dk)
+    dv[...] = jnp.zeros_like(dv)
+    for t in reversed(range(qkv_ref.shape[0])):
+        parts = attend_frame_back(t, qkv_ref, do_ref, full_ref, lse_ref, cos_ref, sin_ref, dk, dv)
+        for i in range(3):
+            out_ref[t, i] = parts[i]
+
+
+def attend_back(qkv, do, full, lse, cos, sin):
+    frames = qkv.shape[0]
+    vmem = pl.BlockSpec(memory_space=pltpu.VMEM)
+    return pl.pallas_call(
+        attend_back_kernel,
+        in_specs=[vmem] * 6,
+        out_specs=vmem,
+        out_shape=jax.ShapeDtypeStruct(qkv.shape, jnp.bfloat16),
+        scratch_shapes=[pltpu.VMEM((frames, HEAD_DIM, TOK), jnp.float32)] * 2,
+        compiler_params=pltpu.CompilerParams(vmem_limit_bytes=32 * 2**20),
+    )(qkv, do, full, lse, cos, sin)
+
+
+TILE = 512
+RING = 4
+
+
+def dotg(left, right, left_dim, right_dim):
+    return lax.dot_general(
+        left, right, (((left_dim,), (right_dim,)), ((), ())), preferred_element_type=jnp.float32
+    )
+
+
+def place_of(start, across, row, col):
+    return start + row * across + col
+
+
+def fetch_tile(places, blocks, held, sem, start, across, row, rows, col, cols):
+    def one(i, carry):
+        r, c = row + i // cols, col + i % cols
+        spot = places[place_of(start, across, r, c)]
+        pltpu.make_async_copy(
+            blocks.at[spread(spot)],
+            held.at[
+                pl.ds(pl.multiple_of(r * BLOCK, BLOCK), BLOCK),
+                pl.ds(pl.multiple_of(c * BLOCK, BLOCK), BLOCK),
+            ],
+            sem,
+        ).start()
+        return carry
+
+    lax.fori_loop(0, rows * cols, one, 0)
+
+
+def fetched(view, sem):
+    pltpu.make_async_copy(view, view, sem).wait()
+
+
+class Outbox:
+    def __init__(self, places, out, stage, sems):
+        self.places, self.out, self.stage, self.sems = places, out, stage, sems
+
+    def put(self, turn, values, start, across, row, col, first):
+        rows, cols = values.shape[0] // BLOCK, values.shape[1] // BLOCK
+        k = turn % RING
+
+        def settle():
+            self.settle(k)
+
+        if first is False:
+            settle()
+        elif first is not True:
+            pl.when(jnp.logical_not(first))(settle)
+        for r in range(rows):
+            for c in range(cols):
+                self.stage[k, r * cols + c] = values[
+                    r * BLOCK : (r + 1) * BLOCK, c * BLOCK : (c + 1) * BLOCK
+                ].astype(jnp.bfloat16)
+
+        def one(i, carry):
+            spot = self.places[place_of(start, across, row + i // cols, col + i % cols)]
+            pltpu.make_async_copy(self.stage.at[k, i], self.out.at[spot], self.sems.at[k]).start()
+            return carry
+
+        lax.fori_loop(0, rows * cols, one, 0)
+
+    def settle(self, k):
+        pltpu.make_async_copy(self.stage.at[k], self.stage.at[k], self.sems.at[k]).wait()
+
+
+def outbox_scratch():
+    return [
+        pltpu.VMEM((RING, (D // BLOCK) * (TILE // BLOCK), BLOCK, BLOCK), jnp.bfloat16),
+        pltpu.SemaphoreType.DMA((RING,)),
+    ]
+
+
+def column_sum(values):
+    return jnp.sum(values, axis=0, keepdims=True)
+
+
+def project_kernel(
+    places, blocks, xt_ref, io_ref, bias_ref, mod_ref, cos_ref, sin_ref, h0_ref, at_ref, out_ref, held, a_ref, sems
+):
+    tiles = 3 * D // TILE
+    for j in range(tiles):
+        fetch_tile(places, blocks, held, sems.at[j], 0, 3 * D // BLOCK, 0, D // BLOCK, j * TILE // BLOCK, TILE // BLOCK)
+    start = dotg(xt_ref[...], io_ref[...], 0, 0) + bias_ref[...]
+    h0_ref[...] = start
+    hat, _ = layer_norm(start)
+    normed = hat * (1 + mod_ref[1:2]) + mod_ref[0:1]
+    a_ref[...] = normed.astype(jnp.bfloat16)
+    at_ref[...] = normed.T.astype(jnp.bfloat16)
+    heads = TILE // HEAD_DIM
+    half = HEAD_DIM // 2
+
+    def one(j, carry):
+        col = pl.multiple_of(j * TILE, TILE)
+        fetched(held.at[:, pl.ds(col, TILE)], sems.at[j])
+        r = matmul(a_ref[...], held[:, pl.ds(col, TILE)]).T
+        kind, head = j // (D // TILE), j % (D // TILE) * heads
+
+        def turned():
+            c, s = cos_ref[...], sin_ref[...]
+            for i in range(heads):
+                first = r[i * HEAD_DIM : i * HEAD_DIM + half]
+                second = r[i * HEAD_DIM + half : (i + 1) * HEAD_DIM]
+                out_ref[head + i, kind, 0:half] = (first * c - second * s).astype(jnp.bfloat16)
+                out_ref[head + i, kind, half:] = (first * s + second * c).astype(jnp.bfloat16)
+
+        def plain():
+            for i in range(heads):
+                out_ref[head + i, kind] = r[i * HEAD_DIM : (i + 1) * HEAD_DIM].astype(jnp.bfloat16)
+
+        pl.when(kind < 2)(turned)
+        pl.when(kind == 2)(plain)
+        return carry
+
+    lax.fori_loop(0, tiles, one, 0)
+
+
+def project(places, blocks, xt, embed, bias, mod, cos, sin):
+    tokens = xt.shape[1]
+    vmem = pl.BlockSpec(memory_space=pltpu.VMEM)
+    return pl.pallas_call(
+        project_kernel,
+        in_specs=[pl.BlockSpec(memory_space=pltpu.SMEM), pl.BlockSpec(memory_space=pl.ANY)] + [vmem] * 6,
+        out_specs=[vmem] * 3,
+        out_shape=[
+            jax.ShapeDtypeStruct((tokens, D), jnp.float32),
+            jax.ShapeDtypeStruct((D, tokens), jnp.bfloat16),
+            jax.ShapeDtypeStruct((HEADS, 3, HEAD_DIM, tokens), jnp.bfloat16),
+        ],
+        scratch_shapes=[
+            pltpu.VMEM((D, 3 * D), jnp.bfloat16),
+            pltpu.VMEM((tokens, D), jnp.bfloat16),
+            pltpu.SemaphoreType.DMA((3 * D // TILE,)),
+        ],
+        compiler_params=pltpu.CompilerParams(vmem_limit_bytes=40 * 2**20),
+    )(places, blocks, xt, embed, bias, mod, cos, sin)
+
+
+GELU_A = math.sqrt(2.0 / math.pi)
+GELU_B = 0.044715
+
+
+def middle_kernel(
+    places, blocks, olt_ref, h0_ref, mod_ref, head_ref, target_ref, scalars,
+    dot_ref, grads_ref, dh1_ref, dhead_ref, dmod_ref, loss_ref,
+    wo, wup, wdown, slope, act, bt, dz_ref, db_ref, h1_ref, y_ref, z_ref, stage, stage_sems, sems,
+):
+    starts, _ = matrix_starts()
+    per = TILE // BLOCK
+    wide = D // BLOCK
+    up_tiles = FFN // TILE
+    fetch_tile(places, blocks, wo, sems.at[0], starts[1], wide, 0, wide, 0, wide)
+    for j in range(up_tiles):
+        fetch_tile(places, blocks, wup, sems.at[1 + j], starts[2], FFN // BLOCK, 0, wide, j * per, per)
+    fetched(wo, sems.at[0])
+    attended = olt_ref[...].astype(jnp.float32).T.astype(jnp.bfloat16)
+    y = matmul(attended, wo[...])
+    y_ref[...] = y
+    h1 = h0_ref[...] + mod_ref[2:3] * y
+    h1_ref[...] = h1
+    hat_two, _ = layer_norm(h1)
+    b32 = hat_two * (1 + mod_ref[4:5]) + mod_ref[3:4]
+    bt[...] = b32.T.astype(jnp.bfloat16)
+    b = b32.astype(jnp.bfloat16)
+    for j in range(up_tiles):
+        fetch_tile(places, blocks, wdown, sems.at[9 + j], starts[3], wide, j * per, per, 0, wide)
+
+    def rise(j, carry):
+        col = pl.multiple_of(j * TILE, TILE)
+        fetched(wup.at[:, pl.ds(col, TILE)], sems.at[1 + j])
+        u = matmul(b, wup[:, pl.ds(col, TILE)])
+        square = u * u
+        t = jnp.tanh(GELU_A * (u + GELU_B * (square * u)))
+        cdf = 0.5 * (1.0 + t)
+        act[:, pl.ds(col, TILE)] = (u * cdf).astype(jnp.bfloat16)
+        slope[:, pl.ds(col, TILE)] = cdf + (0.5 * GELU_A) * u * (1.0 - t * t) * (
+            1.0 + (3.0 * GELU_B) * square
+        )
+        return carry
+
+    lax.fori_loop(0, up_tiles, rise, 0)
+    for j in range(up_tiles):
+        fetched(wdown.at[pl.ds(j * TILE, TILE)], sems.at[9 + j])
+
+    def fall(j, carry):
+        col = pl.multiple_of(j * 256, 256)
+        z_ref[:, pl.ds(col, 256)] = matmul(act[...], wdown[:, pl.ds(col, 256)])
+        return carry
+
+    lax.fori_loop(0, D // 256, fall, 0)
+    z = z_ref[...]
+    h2 = h1_ref[...] + mod_ref[5:6] * z
+    hat_three, inv_three = layer_norm(h2)
+    c = (hat_three * (1 + mod_ref[7:8]) + mod_ref[6:7]).astype(jnp.bfloat16)
+    noised, inv_scale = scalars[0], scalars[1]
+    difference = dotg(head_ref[...], c, 1, 1) - target_ref[...]
+    loss_ref[...] = jnp.full((1, BLOCK), 1.0, jnp.float32) * (
+        jnp.sum(jnp.sum(difference * difference, axis=0, keepdims=True), axis=1, keepdims=True)
+        * (noised * inv_scale)
+    )
+    dpred = (2.0 * inv_scale * noised * difference).astype(jnp.bfloat16)
+    dhead_ref[...] = matmul(dpred, c)
+    dc = dotg(dpred, head_ref[...], 0, 0)
+    dmod_ref[6:7] = column_sum(dc)
+    dmod_ref[7:8] = column_sum(dc * hat_three)
+    dh2 = norm_back(dc * (1 + mod_ref[7:8]), hat_three, inv_three)
+    dmod_ref[5:6] = column_sum(dh2 * z)
+    dz = (dh2 * mod_ref[5:6]).astype(jnp.bfloat16)
+    dz_ref[...] = dz
+    z_ref[...] = dh2
+    db_ref[...] = jnp.zeros_like(db_ref)
+    outbox = Outbox(places, grads_ref, stage, stage_sems)
+
+    def back(j, carry):
+        col = pl.multiple_of(j * TILE, TILE)
+        du = (
+            slope[:, pl.ds(col, TILE)] * dotg(dz_ref[...], wdown[pl.ds(col, TILE)], 1, 1)
+        ).astype(jnp.bfloat16)
+        ddown = dotg(act[:, pl.ds(col, TILE)], dz_ref[...], 0, 0)
+        outbox.put(2 * (j % 2), ddown, starts[3], wide, j * per, 0, j < 2)
+        dup = matmul(bt[...], du)
+        outbox.put(2 * (j % 2) + 1, dup, starts[2], FFN // BLOCK, 0, j * per, j < 2)
+        db_ref[...] += dotg(du, wup[:, pl.ds(col, TILE)], 1, 1)
+        return carry
+
+    lax.fori_loop(0, up_tiles, back, 0)
+    hat_two, inv_two = layer_norm(h1_ref[...])
+    db = db_ref[...]
+    dmod_ref[3:4] = column_sum(db)
+    dmod_ref[4:5] = column_sum(db * hat_two)
+    dh1 = z_ref[...] + norm_back(db * (1 + mod_ref[4:5]), hat_two, inv_two)
+    dh1_ref[...] = dh1
+    dmod_ref[2:3] = column_sum(dh1 * y_ref[...])
+    dmod_ref[0:2] = jnp.zeros((2, D), jnp.float32)
+    dz_ref[...] = (dh1 * mod_ref[2:3]).astype(jnp.bfloat16)
+    for j in range(D // TILE):
+        rows = pl.ds(j * TILE, TILE)
+        dot_ref[rows] = dotg(wo[rows], dz_ref[...], 1, 1).astype(jnp.bfloat16)
+    for j in range(D // TILE):
+        dout = matmul(olt_ref[...], dz_ref[:, j * TILE : (j + 1) * TILE])
+        outbox.put(j, dout, starts[1], wide, 0, j * per, False)
+    for k in range(RING):
+        outbox.settle(k)
+
+
+def middle(places, blocks, olt, h0, mod, head, target, scalars):
+    tokens = h0.shape[0]
+    vmem, smem = pl.BlockSpec(memory_space=pltpu.VMEM), pl.BlockSpec(memory_space=pltpu.SMEM)
+    anyspace = pl.BlockSpec(memory_space=pl.ANY)
+    f32 = jnp.float32
+    return pl.pallas_call(
+        middle_kernel,
+        in_specs=[smem, anyspace] + [vmem] * 5 + [smem],
+        out_specs=[vmem, anyspace] + [vmem] * 4,
+        out_shape=[
+            jax.ShapeDtypeStruct((D, tokens), jnp.bfloat16),
+            jax.ShapeDtypeStruct((matrix_starts()[1], BLOCK, BLOCK), jnp.bfloat16),
+            jax.ShapeDtypeStruct((tokens, D), f32),
+            jax.ShapeDtypeStruct((PIN, D), f32),
+            jax.ShapeDtypeStruct((8, D), f32),
+            jax.ShapeDtypeStruct((1, BLOCK), f32),
+        ],
+        scratch_shapes=[
+            pltpu.VMEM((D, D), jnp.bfloat16),
+            pltpu.VMEM((D, FFN), jnp.bfloat16),
+            pltpu.VMEM((FFN, D), jnp.bfloat16),
+            pltpu.VMEM((tokens, FFN), f32),
+            pltpu.VMEM((tokens, FFN), jnp.bfloat16),
+            pltpu.VMEM((D, tokens), jnp.bfloat16),
+            pltpu.VMEM((tokens, D), jnp.bfloat16),
+            pltpu.VMEM((tokens, D), f32),
+            pltpu.VMEM((tokens, D), f32),
+            pltpu.VMEM((tokens, D), f32),
+            pltpu.VMEM((tokens, D), f32),
+        ]
+        + outbox_scratch()
+        + [pltpu.SemaphoreType.DMA((17,))],
+        compiler_params=pltpu.CompilerParams(vmem_limit_bytes=58 * 2**20),
+    )(places, blocks, olt, h0, mod, head, target, scalars)
+
+
+def final_kernel(
+    places, blocks, drt_ref, at_ref, h0_ref, mod_ref, dh1_ref, xt_ref, grads_in,
+    grads_ref, dmod_ref, dembed_ref, dbias_ref,
+    held, flat, stage, stage_sems, sems,
+):
+    across = 3 * D // BLOCK
+    for j in range(2):
+        fetch_tile(places, blocks, held, sems.at[j], 0, across, j * 4, 4, 0, across)
+    for kind in range(3):
+        for head in range(HEADS):
+            row = kind * D + head * HEAD_DIM
+            flat[row : row + HEAD_DIM] = drt_ref[head, kind]
+    outbox = Outbox(places, grads_ref, stage, stage_sems)
+    for j in range(3 * D // TILE):
+        dw = dotg(at_ref[...], flat[j * TILE : (j + 1) * TILE], 1, 1)
+        outbox.put(j, dw, 0, across, 0, j * TILE // BLOCK, j < RING)
+    for j in range(2):
+        fetched(held.at[pl.ds(j * TILE, TILE)], sems.at[j])
+    da = matmul(held[...], flat[...]).T
+    hat, inverse = layer_norm(h0_ref[...])
+    dmod_ref[0:1] = column_sum(da)
+    dmod_ref[1:2] = column_sum(da * hat)
+    dh0 = (dh1_ref[...] + norm_back(da * (1 + mod_ref[1:2]), hat, inverse)).astype(jnp.bfloat16)
+    dembed_ref[...] = matmul(xt_ref[...], dh0)
+    dbias_ref[...] = column_sum(dh0.astype(jnp.float32))
+    for k in range(RING):
+        outbox.settle(k)
+
+
+def final(places, blocks, drt, at, h0, mod, dh1, xt, grads):
+    vmem, smem = pl.BlockSpec(memory_space=pltpu.VMEM), pl.BlockSpec(memory_space=pltpu.SMEM)
+    anyspace = pl.BlockSpec(memory_space=pl.ANY)
+    f32 = jnp.float32
+    tokens = h0.shape[0]
+    return pl.pallas_call(
+        final_kernel,
+        in_specs=[smem, anyspace] + [vmem] * 6 + [anyspace],
+        out_specs=[anyspace] + [vmem] * 3,
+        out_shape=[
+            jax.ShapeDtypeStruct(grads.shape, grads.dtype),
+            jax.ShapeDtypeStruct((2, D), f32),
+            jax.ShapeDtypeStruct((PIN, D), f32),
+            jax.ShapeDtypeStruct((1, D), f32),
+        ],
+        scratch_shapes=[
+            pltpu.VMEM((D, 3 * D), jnp.bfloat16),
+            pltpu.VMEM((3 * D, tokens), jnp.bfloat16),
+        ]
+        + outbox_scratch()
+        + [pltpu.SemaphoreType.DMA((2,))],
+        input_output_aliases={8: 0},
+        compiler_params=pltpu.CompilerParams(vmem_limit_bytes=40 * 2**20),
+    )(places, blocks, drt, at, h0, mod, dh1, xt, grads)
+
+
+def matrix_starts():
+    starts, total = [], 0
+    for rows_in, cols_in in matrix_shapes():
+        starts.append(total)
+        total += rows_in // BLOCK * (cols_in // BLOCK)
+    return starts, total
+
+
+def spread(place):
+    return place + place // NSLOT
+
+
+def block_places(block_slot):
+    owned = block_slot.reshape(32, -1)
+    ranks = jnp.sum((owned[:, None, :] < owned[:, :, None]).astype(jnp.int32), axis=2)
+    mine = lax.axis_index("frame") * 2 + lax.axis_index("rep")
+    own_ranks = lax.dynamic_index_in_dim(ranks, mine, 0, keepdims=False)
+    counting = jnp.arange(NSLOT, dtype=jnp.int32)
+    perm = jnp.sum(jnp.where(own_ranks[None, :] == counting[:, None], counting[None, :], 0), axis=1)
+    spots = (jnp.arange(32, dtype=jnp.int32)[:, None] * NSLOT + ranks).reshape(-1)
+    natural = jnp.arange(block_slot.shape[0], dtype=jnp.int32)
+    places = jnp.sum(jnp.where(block_slot[None, :] == natural[:, None], spots[None, :], 0), axis=1)
+    return own_ranks, perm, places
+
+
+def rope_columns(frame_ids):
+    pairs = HEAD_DIM // 2
+    time_pairs = pairs // 4
+    row_pairs = (pairs - time_pairs) // 2
+    column_pairs = pairs - time_pairs - row_pairs
+    shape = (frame_ids.shape[0], pairs, GRID * GRID)
+    token = jnp.arange(GRID * GRID, dtype=jnp.int32)
+    groups = (
+        (time_pairs, frame_ids[:, None, None].astype(jnp.float32)),
+        (row_pairs, (token // GRID)[None, None, :].astype(jnp.float32)),
+        (column_pairs, (token % GRID)[None, None, :].astype(jnp.float32)),
+    )
+    angles = jnp.concatenate(
+        [
+            jnp.broadcast_to(pos * frequencies(n)[None, :, None], (shape[0], n, shape[2]))
+            for n, pos in groups
+        ],
+        axis=1,
+    )
+    return (jnp.cos(angles), jnp.sin(angles))
+
+
+def on_grid(
+    clean,
+    noise,
+    levels,
+    flags,
+    frame_map,
+    block_slot,
+    step_count,
+    mat_weight,
+    mat_ema,
+    stat_left,
+    stat_right,
+    root_left,
+    root_right,
+    mod_table,
+    mod_mom,
+    mod_var,
+    mod_ema,
+    io_weight,
+    io_mom,
+    io_var,
+    io_ema,
+):
+    tok_frame = GRID * GRID
+    my_time, my_clip = lax.axis_index("frame"), lax.axis_index("rep")
+    level_here = levels[0, 0] * (1 - flags[0, 0])
+    noised_here = (1 - flags[0, 0]).astype(jnp.float32)
+    fraction = level_here.astype(jnp.float32) / LEVELS
+    frames_in = (
+        jnp.cos(0.5 * jnp.pi * fraction) * clean[0, 0] + jnp.sin(0.5 * jnp.pi * fraction) * noise[0, 0]
+    )
+    noise_high = noise[0, 0].astype(jnp.bfloat16)
+    noise_low = (noise[0, 0] - noise_high.astype(jnp.float32)).astype(jnp.bfloat16)
+    data = jnp.concatenate(
+        [
+            frames_in.astype(jnp.bfloat16).reshape(-1, BLOCK),
+            noise_high.reshape(-1, BLOCK),
+            noise_low.reshape(-1, BLOCK),
+            jnp.full((16, BLOCK), noised_here.astype(jnp.bfloat16)),
+            jnp.full((16, BLOCK), level_here.astype(jnp.bfloat16)),
+        ]
+    )
+    ranks, perm, places = block_places(block_slot)
+    gathered = gather_weights(perm, mat_weight, data)
+    blocks = gathered.reshape(-1, BLOCK, BLOCK)
+    clip_map = lax.dynamic_index_in_dim(frame_map, my_clip, 0, keepdims=False)
+    my_slot = jnp.sum(
+        jnp.where(clip_map == my_time, jnp.arange(clip_map.shape[0], dtype=jnp.int32), 0)
+    )
+    my_data = lax.dynamic_index_in_dim(gathered, my_slot * 2 + my_clip, 0, keepdims=False)[DATA]
+    noised_total = jnp.maximum(jnp.sum(gathered[:, DATA, 96, 0].astype(jnp.float32)), 1.0)
+    noised = my_data[96, 0].astype(jnp.float32)
+    level_now = my_data[112, 0].astype(jnp.int32)
+    inputs = my_data[:32].reshape(PIN, tok_frame)
+    targets = (my_data[32:64].astype(jnp.float32) + my_data[64:96].astype(jnp.float32)).reshape(
+        PIN, tok_frame
+    )
+    modulation = lax.dynamic_index_in_dim(mod_table, level_now, 0, keepdims=False).reshape(8, D)
+    io_low = io_weight.astype(jnp.bfloat16)
+    cosine, sine = rope_columns(jnp.arange(frame_map.shape[1], dtype=jnp.int32))
+    my_cos = lax.dynamic_index_in_dim(cosine, my_time, 0, keepdims=False)
+    my_sin = lax.dynamic_index_in_dim(sine, my_time, 0, keepdims=False)
+    start, normed, parts = project(
+        places, blocks, inputs, io_low[:PIN], io_weight[2 * PIN :], modulation, my_cos, my_sin
+    )
+    mine = lax.all_to_all(parts, "frame", 0, 0, tiled=True)
+    low, full, lse = attend(mine)
+    attended = lax.all_to_all(low, "frame", 0, 0, tiled=True).reshape(D, tok_frame)
+    inv_scale = 1.0 / (noised_total * tok_frame * PIN)
+    grad_heads, grad_blocks, grad_middle, grad_head, grad_mod, loss_part = middle(
+        places,
+        blocks,
+        attended,
+        start,
+        modulation,
+        io_low[PIN : 2 * PIN],
+        targets,
+        jnp.stack([noised, inv_scale]),
+    )
+    grad_mine = lax.all_to_all(
+        grad_heads.reshape(HEADS, HEAD_DIM, tok_frame), "frame", 0, 0, tiled=True
+    )
+    back = attend_back(mine, grad_mine, full, lse, cosine, sine)
+    grad_proj = lax.all_to_all(back, "frame", 0, 0, tiled=True)
+    grad_blocks, grad_mod_one, grad_embed, grad_bias = final(
+        places, blocks, grad_proj, normed, start, modulation, grad_middle, inputs, grad_blocks
+    )
+    row = jnp.concatenate(
+        [
+            grad_mod_one.reshape(-1, BLOCK),
+            grad_mod[2:].reshape(-1, BLOCK),
+            jnp.full((4, BLOCK), level_now.astype(jnp.float32)),
+            jnp.broadcast_to(loss_part, (4, BLOCK)),
+        ]
+    )
+    grad_io = jnp.concatenate(
+        [
+            grad_embed,
+            grad_head,
+            grad_bias,
+            jnp.zeros((SMALL_ROWS - 2 * PIN - 1, D), jnp.float32),
+        ],
+        axis=0,
+    )
+    owned, rows, grad_io = scatter_grads(
+        ranks,
+        grad_blocks.reshape(32, -1, BLOCK, BLOCK),
+        row,
+        grad_io.reshape(SMALL_ROWS, 2, D // 2).swapaxes(0, 1),
+    )
+    grad_io = grad_io.swapaxes(0, 1).reshape(SMALL_ROWS, D)[: 2 * PIN + 1]
+    rows = rows.reshape(32, -1, BLOCK)
+    total_loss = jnp.sum(rows[:, 68, 0])
+    selector = (
+        rows[:, 64, 0].astype(jnp.int32)[None, :] == jnp.arange(LEVELS, dtype=jnp.int32)[:, None]
+    ).astype(jnp.float32)
+    grad_table = jnp.dot(selector, rows[:, :64].reshape(32, 8 * D), precision=TOP_PRECISION)
+    block_limit = CLIP_NORM * BLOCK * NPARAMS ** (-0.5)
+    block_norm = jnp.sqrt(jnp.sum(owned * owned, axis=(1, 2), keepdims=True))
+    mat_grad = owned * (block_limit / jnp.maximum(block_norm, block_limit))
+    grad_norm = jnp.sqrt(jnp.sum(grad_table * grad_table) + jnp.sum(grad_io * grad_io))
+    factor = CLIP_NORM / jnp.maximum(grad_norm, CLIP_NORM)
+    new_mat_weight, new_stat_left, new_stat_right, new_mat_ema = shampoo(
+        mat_grad, mat_weight, mat_ema, stat_left, stat_right, root_left, root_right
+    )
+    step = step_count[0].astype(jnp.float32)
+    new_mod = adamw(grad_table * factor, mod_table, mod_mom, mod_var, mod_ema, step)
+    new_io = adamw(grad_io * factor, io_weight, io_mom, io_var, io_ema, step)
+    return (
+        total_loss * noised_total,
+        noised_total,
+        grad_norm,
+        mat_grad,
+        new_mat_weight,
+        new_stat_left,
+        new_stat_right,
+        new_mat_ema,
+        new_mod[0],
+        new_mod[1],
+        new_mod[2],
+        new_mod[3],
+        new_io[0],
+        new_io[1],
+        new_io[2],
+        new_io[3],
+    )
+
+
 def solution(mesh):
+    tuned = dict(mesh.shape) == {"frame": 16, "rep": 2}
+    body = on_grid if tuned else on_device
     in_specs = (
         P("rep", "frame", None, None),
         P("rep", "frame", None, None),
@@ -561,5 +1802,5 @@
         P(),
     )
     return jax.shard_map(
-        on_device, mesh=mesh, in_specs=in_specs, out_specs=out_specs, check_vma=False
-    )
+        body, mesh=mesh, in_specs=in_specs, out_specs=out_specs, check_vma=False
+    )

time: 1860 us -> 542 us (0.29)
  waiting for transfers between devices: 1060 us -> 40.7 us
  local copies, waits for them, and re-layouts: 419 us -> 21.2 us
  Pallas kernels: 0 us -> 355 us
  matrix products: 120 us -> 17.1 us
  other arithmetic: 99.4 us -> 19.6 us
  blocking collectives: 93.3 us -> 59.6 us
  loops' own time: 29.9 us -> 0 us
    reduce_scatter x2 -> x0, waiting for transfers between devices: 881 us -> none  [the longest x1 455 us: on_device(): lax.psum_scatter(key_terms(lax.axis_size('frame') * local_rows, queries,...]
    pallas_call x0 -> x7, Pallas kernels: none -> 355 us  [the longest x1 122 us: scatter_grads(): pl.pallas_call(scatter_kernel, out_shape=(jax.ShapeDtypeStruct((NSLOT, 12...]
    all_gather x3 -> x0, waiting for transfers between devices: 174 us -> none  [the longest x1 151 us: on_device(): lax.all_gather(mat_weight.astype(jnp.bfloat16), ('frame', 'rep'), axis=0,...]
    scatter x1 -> x0, local copies, waits for them, and re-layouts: 111 us -> none  [on_device(): natural = jnp.zeros_like(gathered).at[block_slot].set(gathered)]
    dot_general x25 -> x1, matrix products: 108 us -> 4.05 us  [on_grid(): jnp.dot(selector, rows[:, :64].reshape(32, 8 * D), precision=TOP_PRECISION)]
    psum x2 -> x0, blocking collectives: 93.3 us -> none  [the longest x1 53 us: on_device(): noised_total = jnp.maximum(lax.psum(jnp.sum(noised), ('frame', 'rep')), 1.0)]
    dynamic_update_slice x16 -> x0, local copies, waits for them, and re-layouts: 80.3 us -> none  [key_terms(): return lax.map(one_block, stacks).reshape(row_count, 2 * D)]
    reshape x7 -> x5, local copies, waits for them, and re-layouts: 65.3 us -> 0.72 us  [the longest x1 0.68 us: on_grid(): grad_io.reshape(SMALL_ROWS, 2, D // 2).swapaxes(0, 1)]
  transfers between devices with their start and end apart: 6 -> 2, of which waited for: 5 -> 2; matrix products, arithmetic and copies ran while one was open for 12% -> 1% of each run, Pallas kernels for 0% -> 0%
where the time goes in v2:
time: 542 us; the launch traced here: 535 us
  Pallas kernels  355 us (65%)
  blocking collectives  59.6 us (11%)
  waiting for transfers between devices  40.7 us (8%)
  local copies, waits for them, and re-layouts  21.2 us (4%)
  other arithmetic  19.6 us (4%)
  matrix products  17.1 us (3%)
  between operations  12 us (2%)
  starting transfers between devices  9.73 us (2%)
    pallas_call x1, Pallas kernels, scatter_grads(): pl.pallas_call(scatter_kernel, out_shape=(jax.ShapeDtypeStruct((NSLOT, 12...  122 us
    pallas_call x1, Pallas kernels, gather_weights(): pl.pallas_call(gather_kernel, out_shape=jax.ShapeDtypeStruct((32, NSLOT +...  109 us
    pallas_call x1, Pallas kernels, middle(): pl.pallas_call(middle_kernel, in_specs=[smem, anyspace] + [vmem] * 5 + [s...  52.8 us
    all_to_all x1, blocking collectives, on_grid(): mine = lax.all_to_all(parts, 'frame', 0, 0, tiled=True)  40.9 us
    all_to_all x1, waiting for transfers between devices, on_grid(): grad_proj = lax.all_to_all(back, 'frame', 0, 0, tiled=True)  31 us
    pallas_call x1, Pallas kernels, attend_back(): pl.pallas_call(attend_back_kernel, in_specs=[vmem] * 6, out_specs=vmem, o...  23.8 us
    pallas_call x1, Pallas kernels, attend(): pl.pallas_call(attend_kernel, in_specs=[vmem], out_specs=[vmem] * 3, out_...  20.8 us
    all_to_all x1, blocking collectives, on_grid(): lax.all_to_all(grad_heads.reshape(HEADS, HEAD_DIM, tok_frame), 'frame', 0...  18.7 us
  transfers between devices with their start and end apart: 2, of which 2 were waited for; matrix products, arithmetic and copies ran while one was open for 1% of the time, Pallas kernels for 0%

profile of v2, /device:TPU:0, one launch (start us, length us, event | category | flops | bytes accessed | tf_op | source)
XLA Modules:
  0.0 535.2 jit_solution(14892046907554019100)
XLA Ops:
  8.1 109.5 %shard_map.324 = bf16[32,25,128,128]{3,2,1,0:T(8,128)(2,1)} custom-call(s32[24]{0:T(128)} %select_reduce_fusion.1.perm_ref, f32[24,128,128]{2,1,0:T(8,128)} %w_ref.1, bf16[128,128]{1,0:T(8,128)(2,1)} %copy-done.36), custom_call_target="tpu_custom_call" | custom-call | tf_op jit(solution)/shard_map/pallas_call | solution.py:740
  121.7 2.0 fusion.4
  126.4 9.6 %shard_map.325 = (f32[256,1024]{1,0:T(8,128)S(1)}, bf16[1024,256]{1,0:T(8,128)(2,1)S(1)}, bf16[16,3,64,256]{3,2,1,0:T(8,128)(2,1)S(1)}) custom-call(s32[768]{0:T(1024)S(1)} %select_reduce_fusion.places, bf16[800,128,128]{2,1,0:T(8,128)(2,1)} %bitcast.62, bf16[16,256]{1,0:T(8,128)(2,1)S(1)} %reshape.296.xt_ref, ...), custom_call_target="tpu_custom_call" | custom-call | tf_op jit(solution)/shard_map/pallas_call | solution.py:1349
  136.1 40.9 %all_to_all.20.qkv_ref = bf16[16,3,64,256]{3,2,1,0:T(8,128)(2,1)S(1)} all-to-all(bf16[16,3,64,256]{3,2,1,0:T(8,128)(2,1)S(1)} %get-tuple-element.35), channel_id=1, replica_groups=mesh['frame'=16,'rep'=2] {'frame'}, dimensions={0} | all-to-all | bytes 3145728 | tf_op jit(solution)/shard_map/all_to_all | solution.py:1677
  177.0 20.8 %shard_map.326 = (bf16[16,64,256]{2,1,0:T(8,128)(2,1)S(1)}, f32[16,64,256]{2,1,0:T(8,128)S(1)}, f32[16,1,256]{2,1,0:T(1,128)S(1)}) custom-call(bf16[16,3,64,256]{3,2,1,0:T(8,128)(2,1)S(1)} %all_to_all.20.qkv_ref), custom_call_target="tpu_custom_call" | custom-call | tf_op jit(solution)/shard_map/pallas_call | solution.py:1192
  199.5 5.3 all-to-all-start.1
  205.5 1.5 convert_reduce_fusion.1
  209.7 9.7 %all-to-all-done.1 = bf16[16,64,256]{2,1,0:T(8,128)(2,1)} async-done(((bf16[16,64,256]{2,1,0:T(8,128)(2,1)}), bf16[16,64,256]{2,1,0:T(8,128)(2,1)}, u32[]{:S(2)}, u32[]{:S(2)}) %all-to-all-start.1) | async-done | bytes 524320 | tf_op jit(solution)/shard_map/all_to_all | solution.py:1679
  219.3 52.8 %shard_map.327 = (bf16[1024,256]{1,0:T(8,128)(2,1)}, bf16[768,128,128]{2,1,0:T(8,128)(2,1)}, f32[256,1024]{1,0:T(8,128)}, f32[16,1024]{1,0:T(8,128)}, f32[8,1024]{1,0:T(8,128)}, /*index=5*/f32[1,128]{1,0:T(1,128)}) custom-call(s32[768]{0:T(1024)} %copy-done.16, bf16[800,128,128]{2,1,0:T(8,128)(2,1)} %bitcast.63, bf16[1024,256]{1,0:T(8,128)(2,1)} %bitcast.11.olt_ref, ...), custom_call_target="tpu_custom_call" | custom-call | tf_op jit(solution)/shard_map/pallas_call | solution.py:1479
  272.1 18.7 %all_to_all.21.do_ref = bf16[16,64,256]{2,1,0:T(8,128)(2,1)S(1)} all-to-all(bf16[16,64,256]{2,1,0:T(8,128)(2,1)} %bitcast.75), channel_id=1, replica_groups=mesh['frame'=16,'rep'=2] {'frame'}, dimensions={0} | all-to-all | bytes 1048576 | tf_op jit(solution)/shard_map/all_to_all | solution.py:1691
  290.9 23.8 %shard_map.328 = bf16[16,3,64,256]{3,2,1,0:T(8,128)(2,1)S(1)} custom-call(bf16[16,3,64,256]{3,2,1,0:T(8,128)(2,1)S(1)} %all_to_all.20.qkv_ref, bf16[16,64,256]{2,1,0:T(8,128)(2,1)S(1)} %all_to_all.21.do_ref, f32[16,64,256]{2,1,0:T(8,128)S(1)} %copy-done.10, f32[16,1,256]{2,1,0:T(1,128)S(1)} %get-tuple-element.40.lse_ref, f32[16,32,256]{2,1,0:T(8,128)S(1)} %copy-done.7, ...), custom_call_target="tpu_custom_call" | custom-call | tf_op jit(solution)/shard_map/pallas_call | solution.py:1218
  315.8 4.4 all-to-all-start.3
  321.2 31.0 %all-to-all-done.3.drt_ref = bf16[16,3,64,256]{3,2,1,0:T(8,128)(2,1)S(1)} async-done(((bf16[16,3,64,256]{3,2,1,0:T(8,128)(2,1)}), bf16[16,3,64,256]{3,2,1,0:T(8,128)(2,1)S(1)}, u32[]{:S(2)}, u32[]{:S(2)}) %all-to-all-start.3) | async-done | bytes 1572896 | tf_op jit(solution)/shard_map/all_to_all | solution.py:1695
  355.7 17.0 %shard_map.329 = (bf16[768,128,128]{2,1,0:T(8,128)(2,1)}, f32[2,1024]{1,0:T(2,128)S(1)}, f32[16,1024]{1,0:T(8,128)S(1)}, f32[1,1024]{1,0:T(1,128)S(1)}) custom-call(s32[768]{0:T(1024)S(1)} %copy-done.17, bf16[800,128,128]{2,1,0:T(8,128)(2,1)} %bitcast.64, bf16[16,3,64,256]{3,2,1,0:T(8,128)(2,1)S(1)} %all-to-all-done.3.drt_ref, ...), custom_call_target="tpu_custom_call", output_to_operand_aliasing={{0}: (8, {})} | custom-call | tf_op jit(solution)/shard_map/pallas_call | solution.py:1544
  374.2 121.9 %shard_map.330 = (f32[24,128,128]{2,1,0:T(8,128)}, f32[2,16,72,128]{3,2,1,0:T(8,128)}, f32[2,40,512]{2,1,0:T(8,128)}) custom-call(s32[24]{0:T(128)} %copy-done.39, bf16[32,24,128,128]{3,2,1,0:T(8,128)(2,1)} %bitcast.65, f32[72,128]{1,0:T(8,128)} %pad_maximum_fusion.1.row_ref, f32[2,40,512]{2,1,0:T(8,128)} %bitcast.69), custom_call_target="tpu_custom_call" | custom-call | tf_op jit(solution)/shard_map/pallas_call | solution.py:1085
  496.1 2.4 slice.74
  498.5 1.6 fusion.15
  500.9 4.1 multiply_reduce_fusion.2
  509.1 1.6 fusion.18
  510.8 2.9 multiply_reduce_fusion
  513.7 4.0 multiply_add_fusion.1
  517.6 4.6 multiply_add_fusion.2
  522.9 4.4 multiply_add_fusion
  528.8 2.6 multiply_add_fusion.3
  (147 shorter events, 26.4 us)
Async XLA Ops:
  0.6 510.1 %copy-start = (f32[24,128,128]{2,1,0:T(8,128)S(1)}, f32[24,128,128]{2,1,0:T(8,128)}, u32[]{:S(2)}) copy-start(f32[24,128,128]{2,1,0:T(8,128)} %param.33) | copy-start | bytes 4718596
  5.3 112.3 %copy-start.39 = (s32[24]{0:T(128)}, s32[24]{0:T(128)S(1)}, u32[]{:S(2)}) copy-start(s32[24]{0:T(128)S(1)} %dynamic-slice_reduce_fusion.1.rank_ref) | copy-start | bytes 292
  8.1 112.2 %copy-start.30 = (f32[33,1024]{1,0:T(8,128)S(1)}, f32[33,1024]{1,0:T(8,128)}, u32[]{:S(2)}) copy-start(f32[33,1024]{1,0:T(8,128)} %param.38) | copy-start | bytes 405508
  117.6 7.9 %copy-start.38 = (s32[768]{0:T(1024)S(1)}, s32[768]{0:T(1024)}, u32[]{:S(2)}) copy-start(s32[768]{0:T(1024)} %param.26) | copy-start | bytes 9220
  121.4 14.6 %copy-start.14 = (f32[8,1024]{1,0:T(8,128)}, f32[8,1024]{1,0:T(8,128)S(1)}, u32[]{:S(2)}) copy-start(f32[8,1024]{1,0:T(8,128)S(1)} %reshape.297.mod_ref) | copy-start | bytes 98308
  125.8 10.2 %copy-start.16 = (s32[768]{0:T(1024)}, s32[768]{0:T(1024)S(1)}, u32[]{:S(2)}) copy-start(s32[768]{0:T(1024)S(1)} %select_reduce_fusion.places) | copy-start | bytes 9220
  136.0 40.9 %copy-start.2 = (f32[256,1024]{1,0:T(8,128)}, f32[256,1024]{1,0:T(8,128)S(1)}, u32[]{:S(2)}) copy-start(f32[256,1024]{1,0:T(8,128)S(1)} %get-tuple-element.37.h0_ref) | copy-start | bytes 3145732
  136.1 40.9 %copy-start.11 = (bf16[1024,256]{1,0:T(8,128)(2,1)}, bf16[1024,256]{1,0:T(8,128)(2,1)S(1)}, u32[]{:S(2)}) copy-start(bf16[1024,256]{1,0:T(8,128)(2,1)S(1)} %get-tuple-element.41.at_ref) | copy-start | bytes 1572868
  199.5 19.8 %all-to-all-start.1 = ((bf16[16,64,256]{2,1,0:T(8,128)(2,1)}), bf16[16,64,256]{2,1,0:T(8,128)(2,1)}, u32[]{:S(2)}, u32[]{:S(2)}) async-start(bf16[16,64,256]{2,1,0:T(8,128)(2,1)} %copy-done.13), calls=%async_computation.1 | async-start | bytes 1048576 | tf_op jit(solution)/shard_map/all_to_all | solution.py:1679
  219.3 71.5 %copy-start.5 = (f32[16,32,256]{2,1,0:T(8,128)S(1)}, f32[16,32,256]{2,1,0:T(8,128)}, u32[]{:S(2)}) copy-start(f32[16,32,256]{2,1,0:T(8,128)} %copy-done.4) | copy-start | bytes 1572868
  219.3 71.5 %copy-start.7 = (f32[16,32,256]{2,1,0:T(8,128)S(1)}, f32[16,32,256]{2,1,0:T(8,128)}, u32[]{:S(2)}) copy-start(f32[16,32,256]{2,1,0:T(8,128)} %copy-done.6) | copy-start | bytes 1572868
  272.1 18.7 %copy-start.10 = (f32[16,64,256]{2,1,0:T(8,128)S(1)}, f32[16,64,256]{2,1,0:T(8,128)}, u32[]{:S(2)}) copy-start(f32[16,64,256]{2,1,0:T(8,128)} %copy-done.9) | copy-start | bytes 3145732
  315.8 5.4 %copy-start.37 = (f32[8,1024]{1,0:T(8,128)S(1)}, f32[8,1024]{1,0:T(8,128)}, u32[]{:S(2)}) copy-start(f32[8,1024]{1,0:T(8,128)} %get-tuple-element.46) | copy-start | bytes 98308
  315.8 36.4 %copy-start.15 = (f32[8,1024]{1,0:T(8,128)S(1)}, f32[8,1024]{1,0:T(8,128)}, u32[]{:S(2)}) copy-start(f32[8,1024]{1,0:T(8,128)} %copy-done.14) | copy-start | bytes 98308
  315.8 36.4 %copy-start.17 = (s32[768]{0:T(1024)S(1)}, s32[768]{0:T(1024)}, u32[]{:S(2)}) copy-start(s32[768]{0:T(1024)} %copy-done.16) | copy-start | bytes 9220
  315.8 36.4 %all-to-all-start.3 = ((bf16[16,3,64,256]{3,2,1,0:T(8,128)(2,1)}), bf16[16,3,64,256]{3,2,1,0:T(8,128)(2,1)S(1)}, u32[]{:S(2)}, u32[]{:S(2)}) async-start(bf16[16,3,64,256]{3,2,1,0:T(8,128)(2,1)} %copy-done.1), calls=%async_computation.3 | async-start | bytes 3145728 | tf_op jit(solution)/shard_map/all_to_all | solution.py:1695
  355.7 17.0 %copy-start.35 = (f32[16,1024]{1,0:T(8,128)S(1)}, f32[16,1024]{1,0:T(8,128)}, u32[]{:S(2)}) copy-start(f32[16,1024]{1,0:T(8,128)} %get-tuple-element.49) | copy-start | bytes 196612
  355.7 17.8 %copy-start.40 = (f32[1,128]{1,0:T(1,128)S(1)}, f32[1,128]{1,0:T(1,128)}, u32[]{:S(2)}) copy-start(f32[1,128]{1,0:T(1,128)} %get-tuple-element.47) | copy-start | bytes 1540
  500.9 5.7 %copy-start.19 = (f32[24,128,128]{2,1,0:T(8,128)S(1)}, f32[24,128,128]{2,1,0:T(8,128)}, u32[]{:S(2)}) copy-start(f32[24,128,128]{2,1,0:T(8,128)} %get-tuple-element.53) | copy-start | bytes 4718596
  509.1 8.5 %copy-start.18 = (f32[24,128,128]{2,1,0:T(8,128)}, f32[24,128,128]{2,1,0:T(8,128)S(1)}, u32[]{:S(2)}) copy-start(f32[24,128,128]{2,1,0:T(8,128)S(1)} %broadcast_multiply_fusion) | copy-start | bytes 4718596
  522.9 5.4 %copy-start.26 = (f32[32,8192]{1,0:T(8,128)S(1)}, f32[32,8192]{1,0:T(8,128)}, u32[]{:S(2)}) copy-start(f32[32,8192]{1,0:T(8,128)} %param.34) | copy-start | bytes 3145732
  522.9 5.4 %copy-start.27 = (f32[32,8192]{1,0:T(8,128)S(1)}, f32[32,8192]{1,0:T(8,128)}, u32[]{:S(2)}) copy-start(f32[32,8192]{1,0:T(8,128)} %param.37) | copy-start | bytes 3145732
  522.9 5.4 %copy-start.28 = (f32[32,8192]{1,0:T(8,128)S(1)}, f32[32,8192]{1,0:T(8,128)}, u32[]{:S(2)}) copy-start(f32[32,8192]{1,0:T(8,128)} %param.36) | copy-start | bytes 3145732
  522.9 5.4 %copy-start.29 = (f32[32,8192]{1,0:T(8,128)S(1)}, f32[32,8192]{1,0:T(8,128)}, u32[]{:S(2)}) copy-start(f32[32,8192]{1,0:T(8,128)} %param.35) | copy-start | bytes 3145732
  (19 other events, 42.5 us)
